TPU v7x, 256 devices: a whole 4x4x8 slice. The times are simulated.
256 devices in a mesh: seq: 8 (over y_lo, x), head: 32 (over z, y_hi, core).
Axes of the slice: x: 4, y: 4 (y_hi: 2, y_lo: 2; y = y_hi * 2 + y_lo), z: 8, core: 2. Of those that a mesh axis runs over, the one named last changes fastest.
Arguments:
- queries: bfloat16 [32, 128, 576], P(None, 'head')
- prompt_latent: bfloat16 [4, 32768, 576], P(None, ('seq', 'head'))
- pool_latent: bfloat16 [512, 64, 576], P(('seq', 'head')), may hold values from -6 to 6
- value_up: bfloat16 [128, 512, 128], P('head'), may hold values from -0.70703125 to 0.70703125
- parents: int32 [32], replicated, may hold values from 0 to 31, as said below
- page_lists: int32 [32, 64], replicated, may hold values from 0 to 511, as said below
- lengths: int32 [32], replicated, may hold values from 2049 to 4096, as said below
Outputs:
- attended: bfloat16 [32, 128, 128], P(None, 'head')
Inputs may be any that keep to these rules, and one draw needn't show every extreme that they name: parents[b] is a beam of the same request: 8 * (b // 8) <= parents[b] < 8 * (b // 8 + 1). `page_lists`: each row holds 64 distinct page numbers; the first 32 of them are the same for all beams of one request. `lengths`: the first beam of each request has 4096 suffix positions.
All inputs are finite; a program needn't handle non-finite values.
Results may differ from a plain program's by a relative error of at most 0.01.
Values may be sent and summed in bfloat16 or wider, within the bound.
A program may use at most 128 MiB of HBM per device.

v0:
```python
import jax
import jax.numpy as jnp
from jax import lax
from jax.sharding import PartitionSpec as P

LAT = 512
ROPE = 64
VDIM = 128
BEAM = 8
PAGE = 64


masked_floor = -1e30


def live_lengths(chosen_pages, chosen_lengths, page_ids):
    slots = jnp.arange(chosen_pages.shape[1], dtype=jnp.int32)
    room = jnp.clip(chosen_lengths[:, None] - slots[None, :] * PAGE, 0, PAGE)
    match = chosen_pages[:, :, None] == page_ids[None, None, :]
    return jnp.sum(jnp.where(match, room[:, :, None], 0), axis=1)


def token_mask(live):
    positions = jnp.arange(PAGE, dtype=jnp.int32)
    return (positions[None, None, :] < live[:, :, None]).reshape(live.shape[0], -1)


def select_parents(parents, page_lists, lengths):
    beams = jnp.arange(parents.shape[0], dtype=jnp.int32)
    picked = parents[:, None] == beams[None, :]
    chosen_pages = jnp.sum(jnp.where(picked[:, :, None], page_lists[None, :, :], 0), axis=1)
    chosen_lengths = jnp.sum(jnp.where(picked, lengths[None, :], 0), axis=1)
    return (chosen_pages, chosen_lengths)


def absorb(running_state, scores, valid, latent_sum):
    peak, totals, running = running_state
    masked = jnp.where(valid, scores, masked_floor)
    new_peak = jnp.maximum(peak, jnp.max(masked, axis=-1))
    keep = jnp.exp(peak - new_peak)
    weights = jnp.where(valid, jnp.exp(masked - new_peak[..., None]), 0.0)
    totals = totals * keep + jnp.sum(weights, axis=-1)
    running = running * keep[..., None] + latent_sum(weights.astype(jnp.bfloat16))
    return (new_peak, totals, running)


def body(queries, prompt_latent, pool_latent, value_up, parents, page_lists, lengths):
    beam_count, heads_dev, width = queries.shape
    requests = prompt_latent.shape[0]
    pages_dev = pool_latent.shape[0]
    scale_factor = (VDIM + ROPE) ** (-0.5)
    chosen_pages, chosen_lengths = select_parents(parents, page_lists, lengths)
    grouped = queries.reshape(requests, BEAM, heads_dev, width)
    group_base = lax.axis_index("seq") * lax.axis_size("head") * pages_dev
    initial = (
        jnp.full((beam_count, heads_dev), masked_floor, jnp.float32),
        jnp.zeros((beam_count, heads_dev), jnp.float32),
        jnp.zeros((beam_count, heads_dev, LAT), jnp.float32),
    )
    shard_rows = lax.all_gather(prompt_latent, "head", axis=1, tiled=True)
    count = shard_rows.shape[1]
    scores = jnp.einsum("rbhc,rnc->rbhn", grouped, shard_rows, preferred_element_type=jnp.float32)
    scores = (scores * scale_factor).reshape(beam_count, heads_dev, count)
    latent_rows = shard_rows[:, :, :LAT]

    def latent_sum(rounded):
        product = jnp.einsum(
            "rbhn,rnl->rbhl",
            rounded.reshape(requests, BEAM, heads_dev, count),
            latent_rows,
            preferred_element_type=jnp.float32,
        )
        return product.reshape(beam_count, heads_dev, LAT)

    partial_state = absorb(initial, scores, jnp.ones((1, 1, 1), dtype=bool), latent_sum)
    shard_pages = lax.all_gather(pool_latent, "head", axis=0, tiled=True)
    suffix_count = shard_pages.shape[0]
    page_ids = group_base + jnp.arange(suffix_count, dtype=jnp.int32)
    valid = token_mask(live_lengths(chosen_pages, chosen_lengths, page_ids))[:, None, :]
    flat_rows = shard_pages.reshape(suffix_count * PAGE, width)
    scores = (
        jnp.einsum("bhc,nc->bhn", queries, flat_rows, preferred_element_type=jnp.float32)
        * scale_factor
    )
    suffix_latent_rows = flat_rows[:, :LAT]

    def latent_sum(rounded):
        return jnp.einsum(
            "bhn,nl->bhl", rounded, suffix_latent_rows, preferred_element_type=jnp.float32
        )

    partial_state = absorb(partial_state, scores, valid, latent_sum)
    peak = partial_state[0]
    top_score = lax.pmax(peak, "seq")
    keep = jnp.exp(peak - top_score)
    totals, running = lax.psum((partial_state[1] * keep, partial_state[2] * keep[..., None]), "seq")
    latent_out = (running / totals[..., None]).astype(jnp.bfloat16)
    attended = jnp.einsum("bhl,hlv->bhv", latent_out, value_up, preferred_element_type=jnp.float32)
    return attended.astype(jnp.bfloat16)


def solution(mesh):
    return jax.shard_map(
        body,
        mesh=mesh,
        in_specs=(
            P(None, "head", None),
            P(None, ("seq", "head"), None),
            P(("seq", "head"), None, None),
            P("head", None, None),
            P(),
            P(),
            P(),
        ),
        out_specs=P(None, "head", None),
        check_vma=False,
    )
```

profile of v0, /device:TPU:8, one launch (start us, length us, event | category | flops | bytes accessed | tf_op | source)
XLA Modules:
  0.0 394.4 jit_solution(3429311660248048590)
XLA Ops:
  6.5 0.0 copy-start
  6.5 0.0 all-gather.5.cloned.1.call-start
  6.5 0.7 all-gather.5.cloned.1.call-update
  7.3 0.0 all-gather.3.cloned.1.call-start
  7.3 0.7 all-gather.3.cloned.1.call-update
  8.0 0.0 all-reduce.2.cloned.1.call-start
  8.1 0.9 select_reduce_fusion.2
  8.9 0.7 iota_compare_fusion
  9.7 0.9 select_reduce_fusion.1
  10.6 0.1 subtract_clamp_fusion
  10.7 0.7 select_reduce_fusion
  11.4 0.3 lt.26
  11.7 0.4 lt.27
  12.1 0.1 lt.24
  12.2 0.1 broadcast_compare_fusion
  12.2 90.5 %all-gather.5.cloned.1.call-done = bf16[64,64,576]{2,1,0:T(8,128)(2,1)} async-done(((bf16[2,64,576]{2,1,0:T(8,128)(2,1)}), bf16[64,64,576]{2,1,0:T(8,128)(2,1)}) %all-gather.5.cloned.1.call-update) | async-done | bytes 4718608 | tf_op jit(solution)/shard_map/all_gather | solution.py:76
  102.8 0.0 copy-done.2
  102.8 5.7 %fusion.28 = (f32[32,4]{0,1:T(4,128)S(1)}, f32[32,4,4096]{2,0,1:T(8,128)}) fusion(bf16[4096,576,1]{1,0,2:T(8,128)(2,1)} %bitcast.47, bf16[32,4,576]{2,1,0:T(4,128)(2,1)S(1)} %copy-done.2, pred[32,4096]{1,0:T(8,128)(4,1)S(1)} %broadcast_compare_fusion), kind=kOutput, calls=%fused_computation.45 | convolution fusion | flops 605552512 | bytes 7094784 | tf_op jit(solution)/shard_map/bhc,nc->bhn/dot_general | solution.py:82
  108.5 158.1 %all-gather.3.cloned.1.call-done = bf16[4,4096,576]{1,2,0:T(8,128)(2,1)} async-done(((bf16[4,128,576]{1,2,0:T(8,128)(2,1)}), bf16[4,4096,576]{1,2,0:T(8,128)(2,1)}) %all-gather.3.cloned.1.call-update) | async-done | bytes 18874384 | tf_op jit(solution)/shard_map/all_gather | solution.py:60
  266.6 8.1 %fusion.27 = (f32[4,8,4]{1,2,0:T(4,128)S(1)}, f32[4,8,4,4096]{3,1,2,0:T(8,128)S(1)}) fusion(bf16[4,4096,576]{1,2,0:T(8,128)(2,1)} %all-gather.3.cloned.1.call-done, bf16[4,8,4,576]{3,2,1,0:T(4,128)(2,1)S(1)} %bitcast.49), kind=kOutput, calls=%fused_computation.44 | convolution fusion | flops 605028224 | bytes 21119488 | tf_op jit(solution)/shard_map/rbhc,rnc->rbhn/dot_general | solution.py:62
  274.7 0.1 max_broadcast_in_dim.20
  274.8 19.5 %pmax.7 = f32[32,4]{0,1:T(4,128)S(1)} all-reduce(f32[32,4]{0,1:T(4,128)S(1)} %max.19), channel_id=1, replica_groups=mesh['seq'=8,'head'=32] {'seq'}, use_global_device_ids=true, to_apply=%region_5.6 | all-reduce | flops 128 | bytes 1024 | tf_op jit(solution)/shard_map/pmax | solution.py:94
  294.3 2.3 fusion.10
  296.7 3.0 fusion.7
  299.6 1.4 fusion.8
  301.0 0.1 reduce_sum.51
  301.1 11.8 %fusion.16 = f32[32,4,512]{2,0,1:T(8,128)} fusion(f32[32,4,512]{2,0,1:T(8,128)S(1)} %fusion.7, bf16[4,4096,576]{1,2,0:T(8,128)(2,1)} %all-gather.3.cloned.1.call-done, bf16[4,8,4,4096]{3,1,2,0:T(8,128)(2,1)} %get-tuple-element.9, f32[32,4]{0,1:T(4,128)S(1)} %get-tuple-element.7, f32[32,4]{0,1:T(4,128)S(1)} %get-tuple-element.6, ...), kind=kOutput, calls=%fused_computation.19 | convolution fusion | flops 537133056 | bytes 18351616 | tf_op jit(solution)/shard_map/rbhn,rnl->rbhl/dot_general | solution.py:67
  312.9 0.0 all-reduce.2.cloned.1.call-update
  312.9 16.0 %psum.15 = f32[32,4]{0,1:T(4,128)S(1)} all-reduce(f32[32,4]{0,1:T(4,128)S(1)} %get-tuple-element.5), channel_id=1, replica_groups=mesh['seq'=8,'head'=32] {'seq'}, use_global_device_ids=true, to_apply=%region_9.10 | all-reduce | flops 128 | bytes 1024 | tf_op jit(solution)/shard_map/psum | solution.py:96
  328.9 57.1 %all-reduce.2.cloned.1.call-done = f32[32,4,512]{2,0,1:T(8,128)} async-done(((f32[32,4,512]{2,0,1:T(8,128)}), f32[32,4,512]{2,0,1:T(8,128)}) %all-reduce.2.cloned.1.call-update) | async-done | bytes 262160 | tf_op jit(solution)/shard_map/psum | solution.py:96
  386.0 1.2 fusion.17
  387.2 0.6 copy.36
  (12 shorter events, 0.1 us)
Async XLA Ops:
  6.5 379.5 %copy-start = (bf16[4,512,128]{2,1,0:T(8,128)(2,1)S(1)}, bf16[4,512,128]{2,1,0:T(8,128)(2,1)}, u32[]{:S(2)}) copy-start(bf16[4,512,128]{2,1,0:T(8,128)(2,1)} %param.10) | copy-start | bytes 1572868
  6.5 96.3 %copy-start.2 = (bf16[32,4,576]{2,1,0:T(4,128)(2,1)S(1)}, bf16[32,4,576]{2,1,0:T(4,128)(2,1)}, u32[]{:S(2)}) copy-start(bf16[32,4,576]{2,1,0:T(4,128)(2,1)} %param.7) | copy-start | bytes 442372
  6.5 96.2 %all-gather.5.cloned.1.call-start = ((), (), s32[]{:S(2)}) async-start(), calls=%async_computation.1 | async-start | bytes 5406720 | tf_op jit(solution)/shard_map/all_gather | solution.py:76
  7.3 259.3 %all-gather.3.cloned.1.call-start = ((), (), s32[]{:S(2)}) async-start(), calls=%async_computation | async-start | bytes 19464192 | tf_op jit(solution)/shard_map/all_gather | solution.py:60
  8.0 378.0 %all-reduce.2.cloned.1.call-start = ((), (), s32[]{:S(2)}) async-start(), calls=%async_computation.2 | async-start | bytes 524288 | tf_op jit(solution)/shard_map/psum | solution.py:96
  294.3 2.3 copy-start.1
Sparse Core Ops, SparseCore 0:
  10.1 92.6 all-gather.4
  105.3 161.2 all-gather.2
  313.0 72.9 all-reduce.1
where the time goes:
time: 395 us; the launch traced here: 394 us
  waiting for transfers between devices  307 us (78%)
  blocking collectives  35.5 us (9%)
  matrix products  29.8 us (8%)
  between operations  13.2 us (3%)
  other arithmetic  7.08 us (2%)
    all_gather x1, waiting for transfers between devices, body(): shard_rows = lax.all_gather(prompt_latent, 'head', axis=1, tiled=True)  158 us
    all_gather x1, waiting for transfers between devices, body(): shard_pages = lax.all_gather(pool_latent, 'head', axis=0, tiled=True)  90.5 us
    psum x1, waiting for transfers between devices, body(): lax.psum((partial_state[1] * keep, partial_state[2] * keep[..., None]), '...  57.1 us
    pmax x1, blocking collectives, body(): top_score = lax.pmax(peak, 'seq')  19.5 us
    psum x1, blocking collectives, body(): lax.psum((partial_state[1] * keep, partial_state[2] * keep[..., None]), '...  16 us
    dot_general x1, matrix products, latent_sum(): jnp.einsum('rbhn,rnl->rbhl', rounded.reshape(requests, BEAM, heads_dev, c...  11.8 us
    dot_general x1, matrix products, body(): jnp.einsum('rbhc,rnc->rbhn', grouped, shard_rows, preferred_element_type=...  8.11 us
  transfers between devices with their start and end apart: 3, of which 3 were waited for; matrix products, arithmetic and copies ran while one was open for 3% of the time, Pallas kernels for 0%

commit v1 on v0

v1 whole, which is shorter than its diff:
```python
import jax
import jax.numpy as jnp
from jax import lax
from jax.experimental import pallas as pl
from jax.experimental.pallas import tpu as pltpu
from jax.sharding import PartitionSpec as P

LAT = 512
ROPE = 64
WIDTH = LAT + ROPE
VDIM = 128
BEAM = 8
PAGE = 64
MAXP = 64
NZ = 8
PACK = LAT + 128
KEYS = 128
LOG2E = 1.4426950408889634
RATE = (VDIM + ROPE) ** -0.5 * LOG2E
MESH = pl.DeviceIdType.MESH
F32 = jnp.float32
BF16 = jnp.bfloat16


def place(x, y, z, c):
    return ((y % 2) * 4 + x, z * 4 + (y // 2) * 2 + c)


def split3(value):
    first = value.astype(BF16).astype(F32)
    rest = value - first
    second = rest.astype(BF16).astype(F32)
    return first, second, rest - second


def pack_stats(peak, total):
    rows = peak.shape[0]
    lane = lax.broadcasted_iota(jnp.int32, (rows, 128), 1)
    out = jnp.zeros((rows, 128), F32)
    for i, term in enumerate((*split3(peak), *split3(total))):
        out = jnp.where(lane == i, term, out)
    return out.astype(BF16)


def unpack_stats(stats):
    stats = stats.astype(F32)
    peak = stats[:, 0:1] + stats[:, 1:2] + stats[:, 2:3]
    total = stats[:, 3:4] + stats[:, 4:5] + stats[:, 5:6]
    return peak, total


def merge(parts):
    stats = [unpack_stats(part[:, LAT:]) for part in parts]
    peak = stats[0][0]
    for other, _ in stats[1:]:
        peak = jnp.maximum(peak, other)
    total = jnp.zeros_like(peak)
    latent = jnp.zeros((peak.shape[0], LAT), F32)
    for part, (part_peak, part_total) in zip(parts, stats):
        keep = jnp.exp2((part_peak - peak) * RATE)
        total = total + part_total * keep
        latent = latent + part[:, :LAT].astype(F32) * keep
    return peak, total, latent


def kernel(
    parents, lengths, page_lists, queries, prompt, pool, value_up,
    out,
    q_buf, k_prompt, k_pool, v_buf, lists, room, cap, scores, probs,
    part, rs1, rs2_src, rs2, out_src,
    local_sem, key_send, key_recv, core_send, core_recv, swap_send, swap_recv, q_send, q_recv,
    rs1_send, rs1_recv, rs2_send, rs2_recv, out_send, out_recv,
):
    seq = lax.axis_index("seq")
    head = lax.axis_index("head")
    x = seq % 4
    y_lo = seq // 4
    c = head % 2
    y_hi = (head // 2) % 2
    z = head // 4
    y = y_hi * 2 + y_lo
    x_hi = x // 2
    x_lo = x % 2
    step = 1 - 2 * c
    request = x_lo * 2 + y_lo

    def shifted(dx, dy, sign=1):
        return place((x + sign * dx + 4) % 4, (y + sign * dy + 4) % 4, z, c)

    other_core = place(x, y, z, 1 - c)
    mirror = place(x, 3 - y, z, c)
    key_moves = ((1, 0), (0, 1), (1, 1))
    scatter_moves = ((2, 0), (0, 2), (2, 2))
    out_moves = [(dx, dy) for dy in range(2) for dx in range(4) if (dx, dy) != (0, 0)]

    def out_place(dx, dy):
        return place((x + dx) % 4, y_hi * 2 + (y_lo + dy) % 2, z, c)

    def out_source(dx, dy):
        return place((x - dx + 4) % 4, y_hi * 2 + (y_lo + dy) % 2, z, c)

    barrier = pltpu.get_barrier_semaphore()
    senders = [shifted(dx * step, dy * step, -1) for dx, dy in key_moves]
    senders += [other_core, mirror]
    senders += [place(x, y, (z + dz) % NZ, c) for dz in range(1, NZ)]
    senders += [shifted(dx, dy) for dx, dy in scatter_moves]
    senders += [out_source(dx, dy) for dx, dy in out_moves]
    for sender in senders:
        pl.semaphore_signal(barrier, inc=1, device_id=sender, device_id_type=MESH)

    own_q = pltpu.make_async_copy(queries.at[request], q_buf.at[y_hi, :, z], local_sem.at[0])
    own_prompt = pltpu.make_async_copy(prompt.at[request], k_prompt.at[c, 0], local_sem.at[1])
    own_pool = pltpu.make_async_copy(pool, k_pool.at[c, 0], local_sem.at[2])
    own_v = pltpu.make_async_copy(value_up, v_buf, local_sem.at[3])
    for copy in (own_q, own_prompt, own_pool, own_v):
        copy.start()

    slot = lax.broadcasted_iota(jnp.int32, (4, MAXP), 1)
    for b in range(BEAM):
        parent = parents[request * BEAM + b]
        lists[4 * b : 4 * b + 4, :] = jnp.broadcast_to(page_lists[pl.ds(parent, 1), :], (4, MAXP))
        room[4 * b : 4 * b + 4, :] = jnp.clip(lengths[parent] - slot * PAGE, 0, PAGE)
    chosen = lists[...]
    space = room[...]
    lane = lax.broadcasted_iota(jnp.int32, (4 * BEAM, KEYS), 1)
    for cc in range(2):
        sign = 1 - 2 * cc
        for kind, (dx, dy) in enumerate(((0, 0),) + key_moves):
            sy = (y - sign * dy + 4) % 4
            s_seq, s_head = place((x - sign * dx + 4) % 4, sy, z, cc)
            page = (s_seq * 32 + s_head) * 2
            live = [
                jnp.sum(jnp.where(chosen == page + i, space, 0), axis=1, keepdims=True) for i in range(2)
            ]
            seen = lane < jnp.where(lane < PAGE, live[0], live[1] + PAGE)
            cap[:, (cc * 4 + kind) * KEYS : (cc * 4 + kind + 1) * KEYS] = jnp.where(seen, jnp.inf, -jnp.inf)

    pl.semaphore_wait(barrier, len(senders))

    copies = []

    def send(src, dst, send_sem, recv_sem, target):
        copy = pltpu.make_async_remote_copy(
            src_ref=src, dst_ref=dst, send_sem=send_sem, recv_sem=recv_sem, device_id=target, device_id_type=MESH
        )
        copy.start()
        copies.append(copy)
        return copy

    mirror_request = x_lo * 2 + 1 - y_lo
    swap = send(queries.at[mirror_request], q_buf.at[y_hi, :, z], swap_send, swap_recv, mirror)
    q_copies = {}
    z_order = (4, 3, 5, 2, 6, 1, 7)
    for dz in z_order:
        q_copies[0, dz] = send(
            queries.at[request], q_buf.at[y_hi, :, z], q_send.at[0, dz], q_recv.at[0, dz],
            place(x, y, (z + dz) % NZ, c),
        )
    key_copies = []
    for i, (dx, dy) in enumerate(key_moves):
        target_request = (x_lo + dx) % 2 * 2 + (y_lo + dy) % 2
        target = shifted(dx * step, dy * step)
        key_copies.append((
            send(prompt.at[target_request], k_prompt.at[c, i + 1], key_send.at[i, 0], key_recv.at[i, 0], target),
            send(pool, k_pool.at[c, i + 1], key_send.at[i, 1], key_recv.at[i, 1], target),
        ))
    core_copies = []

    def to_core(kind, prompt_src, pool_src):
        core_copies.append(send(
            prompt_src, k_prompt.at[c, kind], core_send.at[kind, 0], core_recv.at[kind, 0], other_core))
        core_copies.append(send(
            pool_src, k_pool.at[c, kind], core_send.at[kind, 1], core_recv.at[kind, 1], other_core))

    to_core(0, prompt.at[request], pool)

    swap.wait_recv()
    for dz in z_order:
        q_copies[1, dz] = send(
            q_buf.at[1 - y_hi, :, z], q_buf.at[1 - y_hi, :, z], q_send.at[1, dz], q_recv.at[1, dz],
            place(x, y, (z + dz) % NZ, c),
        )
    for i, (prompt_copy, pool_copy) in enumerate(key_copies):
        prompt_copy.wait_recv()
        pool_copy.wait_recv()
        to_core(i + 1, k_prompt.at[c, i + 1], k_pool.at[c, i + 1])
    own_q.wait()
    own_prompt.wait()
    own_pool.wait()
    for copy in core_copies:
        copy.wait_recv()

    rs1_copies = []

    def attend(group):
        rows = q_buf[group].reshape(2 * KEYS, WIDTH)
        scores[:, : 8 * KEYS] = lax.dot_general(
            rows, k_prompt[...].reshape(8 * KEYS, WIDTH), (((1,), (1,)), ((), ())), preferred_element_type=F32)
        raw = lax.dot_general(
            rows, k_pool[...].reshape(8 * KEYS, WIDTH), (((1,), (1,)), ((), ())), preferred_element_type=F32)
        limit = cap[...].reshape(2, 1, 16, 8 * KEYS)
        raw = jnp.minimum(raw.reshape(2, NZ, 16, 8 * KEYS), limit).reshape(2 * KEYS, 8 * KEYS)
        scores[:, 8 * KEYS :] = raw
        peak = jnp.max(scores[...], axis=1, keepdims=True)
        weights = jnp.exp2((scores[...] - peak) * RATE)
        total = jnp.sum(weights, axis=1, keepdims=True)
        probs[...] = weights.astype(BF16)
        latent = jnp.dot(
            probs[:, : 8 * KEYS], k_prompt[...].reshape(8 * KEYS, WIDTH)[:, :LAT], preferred_element_type=F32)
        latent += jnp.dot(
            probs[:, 8 * KEYS :], k_pool[...].reshape(8 * KEYS, WIDTH)[:, :LAT], preferred_element_type=F32)
        part[group, :, :, :LAT] = latent.astype(BF16).reshape(2, KEYS, LAT)
        part[group, :, :, LAT:] = pack_stats(peak, total).reshape(2, KEYS, 128)

    def scatter(i, group, half):
        dx, dy = scatter_moves[i]
        rs1_copies.append(send(
            part.at[group, half], rs1.at[i], rs1_send.at[i], rs1_recv.at[i], shifted(dx, dy)))

    for dz in z_order:
        q_copies[0, dz].wait_recv()
    attend(y_hi)
    scatter(0, y_hi, 1 - x_hi)
    for dz in z_order:
        q_copies[1, dz].wait_recv()
    attend(1 - y_hi)
    scatter(2, 1 - y_hi, 1 - x_hi)
    scatter(1, 1 - y_hi, x_hi)

    for copy in rs1_copies:
        copy.wait_recv()
    peak, total, latent = merge([part[y_hi, x_hi], rs1[0], rs1[1], rs1[2]])
    rs2_src[:, :, :LAT] = latent.astype(BF16).reshape(NZ, 16, LAT)
    rs2_src[:, :, LAT:] = pack_stats(peak, total).reshape(NZ, 16, 128)
    rs2_copies = []
    for dz in z_order:
        target_z = (z + dz) % NZ
        rs2_copies.append(send(
            rs2_src.at[target_z], rs2.at[dz], rs2_send.at[dz], rs2_recv.at[dz], place(x, y, target_z, c)))
    rs2[0] = rs2_src[z]
    own_v.wait()
    for copy in rs2_copies:
        copy.wait_recv()
    peak, total, latent = merge([rs2[i] for i in range(NZ)])
    latent = (latent / total).astype(BF16)
    row = lax.broadcasted_iota(jnp.int32, (16, VDIM), 0) % 4
    attended = jnp.zeros((16, VDIM), F32)
    for h in range(4):
        product = jnp.dot(latent, v_buf[h], preferred_element_type=F32)
        attended = jnp.where(row == h, product, attended)
    out_src[...] = attended.astype(BF16)
    place_out = request * 2 + x_hi
    out_copies = []
    for i, (dx, dy) in enumerate(out_moves):
        out_copies.append(send(
            out_src, out.at[place_out], out_send.at[i], out_recv.at[i], out_place(dx, dy)))
    out[place_out] = out_src[...]
    for copy in out_copies:
        copy.wait_recv()
    for copy in copies:
        copy.wait_send()


def body(queries, prompt_latent, pool_latent, value_up, parents, page_lists, lengths):
    vmem = pl.BlockSpec(memory_space=pltpu.VMEM)
    smem = pl.BlockSpec(memory_space=pltpu.SMEM)
    hbm = pl.BlockSpec(memory_space=pl.ANY)
    dma = pltpu.SemaphoreType.DMA
    result = pl.pallas_call(
        kernel,
        out_shape=jax.ShapeDtypeStruct((8, 16, VDIM), BF16),
        in_specs=[smem, smem, vmem, hbm, hbm, hbm, hbm],
        out_specs=vmem,
        scratch_shapes=[
            pltpu.VMEM((2, 2, NZ, 16, WIDTH), BF16),
            pltpu.VMEM((2, 4, KEYS, WIDTH), BF16),
            pltpu.VMEM((2, 4, 2, PAGE, WIDTH), BF16),
            pltpu.VMEM((4, LAT, VDIM), BF16),
            pltpu.VMEM((4 * BEAM, MAXP), jnp.int32),
            pltpu.VMEM((4 * BEAM, MAXP), jnp.int32),
            pltpu.VMEM((4 * BEAM, 8 * KEYS), F32),
            pltpu.VMEM((2 * KEYS, 16 * KEYS), F32),
            pltpu.VMEM((2 * KEYS, 16 * KEYS), BF16),
            pltpu.VMEM((2, 2, KEYS, PACK), BF16),
            pltpu.VMEM((3, KEYS, PACK), BF16),
            pltpu.VMEM((NZ, 16, PACK), BF16),
            pltpu.VMEM((NZ, 16, PACK), BF16),
            pltpu.VMEM((16, VDIM), BF16),
            dma((4,)), dma((3, 2)), dma((3, 2)), dma((4, 2)), dma((4, 2)), dma, dma, dma((2, NZ)), dma((2, NZ)),
            dma((3,)), dma((3,)), dma((NZ,)), dma((NZ,)), dma((7,)), dma((7,)),
        ],
        compiler_params=pltpu.CompilerParams(
            collective_id=0, has_side_effects=True, vmem_limit_bytes=48 * 2**20
        ),
    )(
        parents, lengths, page_lists, queries.reshape(4, 2, 16, WIDTH), prompt_latent, pool_latent, value_up
    )
    return result.reshape(32, 4, VDIM)


def solution(mesh):
    return jax.shard_map(
        body,
        mesh=mesh,
        in_specs=(
            P(None, "head", None),
            P(None, ("seq", "head"), None),
            P(("seq", "head"), None, None),
            P("head", None, None),
            P(),
            P(),
            P(),
        ),
        out_specs=P(None, "head", None),
        check_vma=False,
    )
```

time: 395 us -> 51.1 us (0.13)
  waiting for transfers between devices: 307 us -> 0 us
  Pallas kernels: 0 us -> 47.8 us
  blocking collectives: 35.5 us -> 0 us
  matrix products: 29.8 us -> 0 us
  between operations: 13.2 us -> 0.1 us
  other arithmetic: 7.08 us -> 0 us
    all_gather x2 -> x0, waiting for transfers between devices: 249 us -> none  [the longest x1 158 us: body(): shard_rows = lax.all_gather(prompt_latent, 'head', axis=1, tiled=True)]
    psum x1 -> x0, waiting for transfers between devices: 57.1 us -> none  [body(): lax.psum((partial_state[1] * keep, partial_state[2] * keep[..., None]), '...]
    pallas_call x0 -> x1, Pallas kernels: none -> 47.8 us  [body(): pl.pallas_call(kernel, out_shape=jax.ShapeDtypeStruct((8, 16, VDIM), BF16...]
    dot_general x5 -> x0, matrix products: 29.8 us -> none  [the longest x1 11.8 us: latent_sum(): jnp.einsum('rbhn,rnl->rbhl', rounded.reshape(requests, BEAM, heads_dev, c...]
    pmax x1 -> x0, blocking collectives: 19.5 us -> none  [body(): top_score = lax.pmax(peak, 'seq')]
    psum x1 -> x0, blocking collectives: 16 us -> none  [body(): lax.psum((partial_state[1] * keep, partial_state[2] * keep[..., None]), '...]
    reduce_sum x5 -> x0, other arithmetic: 6.17 us -> none  [the longest x2 3.68 us: absorb(): totals = totals * keep + jnp.sum(weights, axis=-1)]
  transfers between devices with their start and end apart: 3 -> 0, of which waited for: 3 -> 0; matrix products, arithmetic and copies ran while one was open for 3% -> 0% of each run, Pallas kernels for 0% -> 0%
where the time goes in v1:
time: 51.1 us; the launch traced here: 51 us
  Pallas kernels  47.8 us (94%)
  local copies, waits for them, and re-layouts  3.05 us (6%)
    pallas_call x1, Pallas kernels, body(): pl.pallas_call(kernel, out_shape=jax.ShapeDtypeStruct((8, 16, VDIM), BF16...  47.8 us
    unnamed x12, local copies, waits for them, and re-layouts  2.06 us

profile of v1, /device:TPU:8, one launch (start us, length us, event | category | flops | bytes accessed | tf_op | source)
XLA Modules:
  0.0 51.0 jit_solution(3793171314043900689)
XLA Ops:
  0.0 1.0 %reshape.6.queries = bf16[4,2,16,576]{3,2,1,0:T(8,128)(2,1)S(1)} reshape(bf16[32,4,576]{2,1,0:T(4,128)(2,1)} %param.7) | data formatting | bytes 294912 | tf_op jit(solution)/shard_map/reshape | solution.py:296
  1.0 0.0 copy-start
  1.0 0.0 copy-start.1
  1.0 0.0 copy-start.2
  1.0 0.0 copy-start.3
  1.0 0.0 copy-start.4
  1.1 1.4 %copy.8.prompt = bf16[4,128,576]{2,1,0:T(8,128)(2,1)S(1)} copy(bf16[4,128,576]{1,2,0:T(8,128)(2,1)} %param.8) | data formatting | bytes 1179648 | tf_op args[1]
  2.5 0.0 copy-done
  2.5 0.0 copy-done.1
  2.5 0.0 copy-done.2
  2.5 0.0 copy-done.3
  2.5 0.0 copy-done.4
  2.5 47.8 %shard_map.73 = bf16[8,16,128]{2,1,0:T(8,128)(2,1)S(1)} custom-call(s32[32]{0:T(128)S(1)} %copy-done.3, s32[32]{0:T(128)S(1)} %copy-done.4, s32[32,64]{1,0:T(8,128)S(1)} %copy-done.2, bf16[4,2,16,576]{3,2,1,0:T(8,128)(2,1)S(1)} %reshape.6.queries, bf16[4,128,576]{2,1,0:T(8,128)(2,1)S(1)} %copy.8.prompt, bf16[2,64,576]{2,1,0:T(8,128)(2,1)S(1)} %copy-done.1, ...), custom_call_target="tpu_custom_call" | custom-call | tf_op jit(solution)/shard_map/pallas_call | solution.py:269
  50.3 0.6 %copy.10 = bf16[32,4,128]{2,1,0:T(4,128)(2,1)} copy(bf16[32,4,128]{2,1,0:T(4,128)(2,1)S(1)} %bitcast.1) | data formatting | bytes 65536
Async XLA Ops:
  1.0 1.5 %copy-start = (bf16[4,512,128]{2,1,0:T(8,128)(2,1)S(1)}, bf16[4,512,128]{2,1,0:T(8,128)(2,1)}, u32[]{:S(2)}) copy-start(bf16[4,512,128]{2,1,0:T(8,128)(2,1)} %value_up.1) | copy-start | bytes 1572868
  1.0 1.5 %copy-start.1 = (bf16[2,64,576]{2,1,0:T(8,128)(2,1)S(1)}, bf16[2,64,576]{2,1,0:T(8,128)(2,1)}, u32[]{:S(2)}) copy-start(bf16[2,64,576]{2,1,0:T(8,128)(2,1)} %pool.1) | copy-start | bytes 442372
  1.0 1.5 %copy-start.2 = (s32[32,64]{1,0:T(8,128)S(1)}, s32[32,64]{1,0:T(8,128)}, u32[]{:S(2)}) copy-start(s32[32,64]{1,0:T(8,128)} %page_lists.1) | copy-start | bytes 24580
  1.0 1.5 %copy-start.3 = (s32[32]{0:T(128)S(1)}, s32[32]{0:T(128)}, u32[]{:S(2)}) copy-start(s32[32]{0:T(128)} %parents.1) | copy-start | bytes 388
  1.0 1.5 %copy-start.4 = (s32[32]{0:T(128)S(1)}, s32[32]{0:T(128)}, u32[]{:S(2)}) copy-start(s32[32]{0:T(128)} %lengths.1) | copy-start | bytes 388

commit v2 on v1

--- a/solution.py
+++ b/solution.py
@@ -49,8 +49,7 @@
     return peak, total
 
 
-def merge(parts):
-    stats = [unpack_stats(part[:, LAT:]) for part in parts]
+def merge(parts, stats):
     peak = stats[0][0]
     for other, _ in stats[1:]:
         peak = jnp.maximum(peak, other)
@@ -66,8 +65,8 @@
 def kernel(
     parents, lengths, page_lists, queries, prompt, pool, value_up,
     out,
-    q_buf, k_prompt, k_pool, v_buf, lists, room, cap, scores, probs,
-    part, rs1, rs2_src, rs2, out_src,
+    q_in, q_wide, q_mirror, q_buf, pool_in, keys, v_buf, lists, room, cap, scores, probs,
+    part, stat, rs1, rs1_stat, rs2_src, rs2, out_src,
     local_sem, key_send, key_recv, core_send, core_recv, swap_send, swap_recv, q_send, q_recv,
     rs1_send, rs1_recv, rs2_send, rs2_recv, out_send, out_recv,
 ):
@@ -108,12 +107,69 @@
     for sender in senders:
         pl.semaphore_signal(barrier, inc=1, device_id=sender, device_id_type=MESH)
 
-    own_q = pltpu.make_async_copy(queries.at[request], q_buf.at[y_hi, :, z], local_sem.at[0])
-    own_prompt = pltpu.make_async_copy(prompt.at[request], k_prompt.at[c, 0], local_sem.at[1])
-    own_pool = pltpu.make_async_copy(pool, k_pool.at[c, 0], local_sem.at[2])
-    own_v = pltpu.make_async_copy(value_up, v_buf, local_sem.at[3])
-    for copy in (own_q, own_prompt, own_pool, own_v):
+    mirror_request = x_lo * 2 + 1 - y_lo
+    own_q = pltpu.make_async_copy(queries.at[pl.ds(request * BEAM, BEAM)], q_in.at[0], local_sem.at[0])
+    mirror_q = pltpu.make_async_copy(queries.at[pl.ds(mirror_request * BEAM, BEAM)], q_in.at[1], local_sem.at[1])
+    own_pool = pltpu.make_async_copy(pool, pool_in, local_sem.at[2])
+    own_prompt = pltpu.make_async_copy(prompt.at[request], keys.at[c, 0, 0], local_sem.at[3])
+    own_v = pltpu.make_async_copy(value_up, v_buf, local_sem.at[4])
+    own_q.start()
+    mirror_q.start()
+    own_pool.start()
+    own_prompt.start()
+    own_v.start()
+
+    def packed(i):
+        for b in range(BEAM):
+            block = q_in[i, b].astype(F32)
+            half, start = b // 4, b % 4 * 4
+            q_wide[i, start : start + 4, half * LAT : (half + 1) * LAT] = block[:, :LAT]
+            if half:
+                rotary = jnp.concatenate([q_in[i, b - 4].astype(F32)[:, LAT:], block[:, LAT:]], axis=1)
+                q_wide[i, start : start + 4, 2 * LAT :] = rotary
+        return q_wide[i].astype(BF16)
+
+    mirror_q.wait()
+    q_mirror[...] = packed(1)
+    own_q.wait()
+    q_buf[y_hi, z] = packed(0)
+    own_pool.wait()
+    flat_pool = pool_in[...].reshape(KEYS, WIDTH)
+    keys[c, 0, 1, :LAT] = flat_pool[:, :LAT].T
+    keys[c, 0, 1, LAT:] = flat_pool[:, LAT:].T
+
+    pl.semaphore_wait(barrier, len(senders))
+
+    copies = []
+
+    def send(src, dst, send_sem, recv_sem, target):
+        copy = pltpu.make_async_remote_copy(
+            src_ref=src, dst_ref=dst, send_sem=send_sem, recv_sem=recv_sem, device_id=target, device_id_type=MESH
+        )
         copy.start()
+        copies.append(copy)
+        return copy
+
+    swap = send(q_mirror, q_buf.at[y_hi, z], swap_send, swap_recv, mirror)
+    q_copies = {}
+    far = (4, 3, 5)
+    near = (2, 6, 1, 7)
+    for dz in far + near:
+        q_copies[0, dz] = send(
+            q_buf.at[y_hi, z], q_buf.at[y_hi, z], q_send.at[0, dz], q_recv.at[0, dz],
+            place(x, y, (z + dz) % NZ, c),
+        )
+    key_copies = []
+    for i, (dx, dy) in enumerate(key_moves):
+        target_request = (x_lo + dx) % 2 * 2 + (y_lo + dy) % 2
+        target = shifted(dx * step, dy * step)
+        key_copies.append((
+            send(prompt.at[target_request], keys.at[c, i + 1, 0], key_send.at[i, 0], key_recv.at[i, 0], target),
+            send(keys.at[c, 0, 1], keys.at[c, i + 1, 1], key_send.at[i, 1], key_recv.at[i, 1], target),
+        ))
+    own_prompt.wait()
+    core_copies = [
+        send(keys.at[c, 0], keys.at[c, 0], core_send.at[0], core_recv.at[0], other_core)]
 
     slot = lax.broadcasted_iota(jnp.int32, (4, MAXP), 1)
     for b in range(BEAM):
@@ -135,93 +191,69 @@
             seen = lane < jnp.where(lane < PAGE, live[0], live[1] + PAGE)
             cap[:, (cc * 4 + kind) * KEYS : (cc * 4 + kind + 1) * KEYS] = jnp.where(seen, jnp.inf, -jnp.inf)
 
-    pl.semaphore_wait(barrier, len(senders))
-
-    copies = []
-
-    def send(src, dst, send_sem, recv_sem, target):
-        copy = pltpu.make_async_remote_copy(
-            src_ref=src, dst_ref=dst, send_sem=send_sem, recv_sem=recv_sem, device_id=target, device_id_type=MESH
-        )
-        copy.start()
-        copies.append(copy)
-        return copy
-
-    mirror_request = x_lo * 2 + 1 - y_lo
-    swap = send(queries.at[mirror_request], q_buf.at[y_hi, :, z], swap_send, swap_recv, mirror)
-    q_copies = {}
-    z_order = (4, 3, 5, 2, 6, 1, 7)
-    for dz in z_order:
-        q_copies[0, dz] = send(
-            queries.at[request], q_buf.at[y_hi, :, z], q_send.at[0, dz], q_recv.at[0, dz],
+    swap.wait_recv()
+    for dz in near:
+        q_copies[1, dz] = send(
+            q_buf.at[1 - y_hi, z], q_buf.at[1 - y_hi, z], q_send.at[1, dz], q_recv.at[1, dz],
             place(x, y, (z + dz) % NZ, c),
         )
-    key_copies = []
-    for i, (dx, dy) in enumerate(key_moves):
-        target_request = (x_lo + dx) % 2 * 2 + (y_lo + dy) % 2
-        target = shifted(dx * step, dy * step)
-        key_copies.append((
-            send(prompt.at[target_request], k_prompt.at[c, i + 1], key_send.at[i, 0], key_recv.at[i, 0], target),
-            send(pool, k_pool.at[c, i + 1], key_send.at[i, 1], key_recv.at[i, 1], target),
-        ))
-    core_copies = []
-
-    def to_core(kind, prompt_src, pool_src):
-        core_copies.append(send(
-            prompt_src, k_prompt.at[c, kind], core_send.at[kind, 0], core_recv.at[kind, 0], other_core))
-        core_copies.append(send(
-            pool_src, k_pool.at[c, kind], core_send.at[kind, 1], core_recv.at[kind, 1], other_core))
-
-    to_core(0, prompt.at[request], pool)
-
-    swap.wait_recv()
-    for dz in z_order:
+    for dz in far:
+        q_copies[0, dz].wait_recv()
+        source = (z - dz + NZ) % NZ
         q_copies[1, dz] = send(
-            q_buf.at[1 - y_hi, :, z], q_buf.at[1 - y_hi, :, z], q_send.at[1, dz], q_recv.at[1, dz],
-            place(x, y, (z + dz) % NZ, c),
-        )
+            q_buf.at[y_hi, source], q_buf.at[y_hi, source], q_send.at[1, dz], q_recv.at[1, dz], shifted(0, 2))
     for i, (prompt_copy, pool_copy) in enumerate(key_copies):
         prompt_copy.wait_recv()
         pool_copy.wait_recv()
-        to_core(i + 1, k_prompt.at[c, i + 1], k_pool.at[c, i + 1])
-    own_q.wait()
-    own_prompt.wait()
-    own_pool.wait()
+        core_copies.append(send(
+            keys.at[c, i + 1], keys.at[c, i + 1], core_send.at[i + 1], core_recv.at[i + 1], other_core))
     for copy in core_copies:
         copy.wait_recv()
 
+    key_blocks = [(cc, kind, pooled) for pooled in range(2) for cc in range(2) for kind in range(4)]
+
     rs1_copies = []
 
     def attend(group):
-        rows = q_buf[group].reshape(2 * KEYS, WIDTH)
-        scores[:, : 8 * KEYS] = lax.dot_general(
-            rows, k_prompt[...].reshape(8 * KEYS, WIDTH), (((1,), (1,)), ((), ())), preferred_element_type=F32)
-        raw = lax.dot_general(
-            rows, k_pool[...].reshape(8 * KEYS, WIDTH), (((1,), (1,)), ((), ())), preferred_element_type=F32)
-        limit = cap[...].reshape(2, 1, 16, 8 * KEYS)
-        raw = jnp.minimum(raw.reshape(2, NZ, 16, 8 * KEYS), limit).reshape(2 * KEYS, 8 * KEYS)
-        scores[:, 8 * KEYS :] = raw
+        block = q_buf[group].reshape(KEYS, 2 * LAT + 128)
+        rotary = block[:, 2 * LAT :]
+        lane = lax.broadcasted_iota(jnp.int32, (KEYS, 128), 1)
+        rows = jnp.concatenate([
+            jnp.concatenate([block[:, :LAT], jnp.where(lane < ROPE, rotary, 0)], axis=1),
+            jnp.concatenate([block[:, LAT : 2 * LAT], jnp.where(lane < ROPE, 0, rotary)], axis=1),
+        ], axis=0)
+        for pair in range(8):
+            columns = jnp.concatenate([keys[k] for k in key_blocks[2 * pair : 2 * pair + 2]], axis=1)
+            columns = jnp.concatenate([columns, columns[LAT:]], axis=0)
+            raw = jnp.dot(rows, columns, preferred_element_type=F32)
+            if pair >= 4:
+                limit = cap[:, (2 * pair - 8) * KEYS : (2 * pair - 6) * KEYS].reshape(2, 1, 16, 2 * KEYS)
+                raw = jnp.minimum(raw.reshape(2, NZ, 16, 2 * KEYS), limit).reshape(2 * KEYS, 2 * KEYS)
+            scores[:, 2 * pair * KEYS : 2 * (pair + 1) * KEYS] = raw
         peak = jnp.max(scores[...], axis=1, keepdims=True)
         weights = jnp.exp2((scores[...] - peak) * RATE)
         total = jnp.sum(weights, axis=1, keepdims=True)
         probs[...] = weights.astype(BF16)
-        latent = jnp.dot(
-            probs[:, : 8 * KEYS], k_prompt[...].reshape(8 * KEYS, WIDTH)[:, :LAT], preferred_element_type=F32)
-        latent += jnp.dot(
-            probs[:, 8 * KEYS :], k_pool[...].reshape(8 * KEYS, WIDTH)[:, :LAT], preferred_element_type=F32)
-        part[group, :, :, :LAT] = latent.astype(BF16).reshape(2, KEYS, LAT)
-        part[group, :, :, LAT:] = pack_stats(peak, total).reshape(2, KEYS, 128)
+        values = jnp.concatenate([keys[cc, kind, pooled, :LAT] for cc, kind, pooled in key_blocks], axis=1)
+        latent = lax.dot_general(
+            probs[...], values, (((1,), (1,)), ((), ())), preferred_element_type=F32)
+        part[group] = latent.astype(BF16).reshape(2, KEYS, LAT)
+        for half in range(2):
+            half_rows = slice(half * KEYS, (half + 1) * KEYS)
+            stat[group, half] = jnp.where(lane == 0, peak[half_rows], total[half_rows]).T[:8]
 
     def scatter(i, group, half):
         dx, dy = scatter_moves[i]
         rs1_copies.append(send(
-            part.at[group, half], rs1.at[i], rs1_send.at[i], rs1_recv.at[i], shifted(dx, dy)))
-
-    for dz in z_order:
+            part.at[group, half], rs1.at[i], rs1_send.at[i, 0], rs1_recv.at[i, 0], shifted(dx, dy)))
+        rs1_copies.append(send(
+            stat.at[group, half], rs1_stat.at[i], rs1_send.at[i, 1], rs1_recv.at[i, 1], shifted(dx, dy)))
+
+    for dz in near:
         q_copies[0, dz].wait_recv()
     attend(y_hi)
     scatter(0, y_hi, 1 - x_hi)
-    for dz in z_order:
+    for dz in near + far:
         q_copies[1, dz].wait_recv()
     attend(1 - y_hi)
     scatter(2, 1 - y_hi, 1 - x_hi)
@@ -229,11 +261,15 @@
 
     for copy in rs1_copies:
         copy.wait_recv()
-    peak, total, latent = merge([part[y_hi, x_hi], rs1[0], rs1[1], rs1[2]])
+    columns = jnp.concatenate([
+        stat[y_hi, x_hi], rs1_stat[0], rs1_stat[1], rs1_stat[2], jnp.zeros((KEYS - 32, KEYS), F32)], axis=0).T
+    peak, total, latent = merge(
+        [part[y_hi, x_hi], rs1[0], rs1[1], rs1[2]],
+        [(columns[:, 8 * i : 8 * i + 1], columns[:, 8 * i + 1 : 8 * i + 2]) for i in range(4)])
     rs2_src[:, :, :LAT] = latent.astype(BF16).reshape(NZ, 16, LAT)
     rs2_src[:, :, LAT:] = pack_stats(peak, total).reshape(NZ, 16, 128)
     rs2_copies = []
-    for dz in z_order:
+    for dz in far + near:
         target_z = (z + dz) % NZ
         rs2_copies.append(send(
             rs2_src.at[target_z], rs2.at[dz], rs2_send.at[dz], rs2_recv.at[dz], place(x, y, target_z, c)))
@@ -241,7 +277,8 @@
     own_v.wait()
     for copy in rs2_copies:
         copy.wait_recv()
-    peak, total, latent = merge([rs2[i] for i in range(NZ)])
+    blocks = [rs2[i] for i in range(NZ)]
+    peak, total, latent = merge(blocks, [unpack_stats(block[:, LAT:]) for block in blocks])
     latent = (latent / total).astype(BF16)
     row = lax.broadcasted_iota(jnp.int32, (16, VDIM), 0) % 4
     attended = jnp.zeros((16, VDIM), F32)
@@ -272,28 +309,33 @@
         in_specs=[smem, smem, vmem, hbm, hbm, hbm, hbm],
         out_specs=vmem,
         scratch_shapes=[
-            pltpu.VMEM((2, 2, NZ, 16, WIDTH), BF16),
-            pltpu.VMEM((2, 4, KEYS, WIDTH), BF16),
-            pltpu.VMEM((2, 4, 2, PAGE, WIDTH), BF16),
+            pltpu.VMEM((2, BEAM, 4, WIDTH), BF16),
+            pltpu.VMEM((2, 16, 2 * LAT + 128), F32),
+            pltpu.VMEM((16, 2 * LAT + 128), BF16),
+            pltpu.VMEM((2, NZ, 16, 2 * LAT + 128), BF16),
+            pltpu.VMEM((2, PAGE, WIDTH), BF16),
+            pltpu.VMEM((2, 4, 2, WIDTH, KEYS), BF16),
             pltpu.VMEM((4, LAT, VDIM), BF16),
             pltpu.VMEM((4 * BEAM, MAXP), jnp.int32),
             pltpu.VMEM((4 * BEAM, MAXP), jnp.int32),
             pltpu.VMEM((4 * BEAM, 8 * KEYS), F32),
             pltpu.VMEM((2 * KEYS, 16 * KEYS), F32),
             pltpu.VMEM((2 * KEYS, 16 * KEYS), BF16),
-            pltpu.VMEM((2, 2, KEYS, PACK), BF16),
-            pltpu.VMEM((3, KEYS, PACK), BF16),
+            pltpu.VMEM((2, 2, KEYS, LAT), BF16),
+            pltpu.VMEM((2, 2, 8, KEYS), F32),
+            pltpu.VMEM((3, KEYS, LAT), BF16),
+            pltpu.VMEM((3, 8, KEYS), F32),
             pltpu.VMEM((NZ, 16, PACK), BF16),
             pltpu.VMEM((NZ, 16, PACK), BF16),
             pltpu.VMEM((16, VDIM), BF16),
-            dma((4,)), dma((3, 2)), dma((3, 2)), dma((4, 2)), dma((4, 2)), dma, dma, dma((2, NZ)), dma((2, NZ)),
-            dma((3,)), dma((3,)), dma((NZ,)), dma((NZ,)), dma((7,)), dma((7,)),
+            dma((5,)), dma((3, 2)), dma((3, 2)), dma((4,)), dma((4,)), dma, dma, dma((2, NZ)), dma((2, NZ)),
+            dma((3, 2)), dma((3, 2)), dma((NZ,)), dma((NZ,)), dma((7,)), dma((7,)),
         ],
         compiler_params=pltpu.CompilerParams(
-            collective_id=0, has_side_effects=True, vmem_limit_bytes=48 * 2**20
+            collective_id=0, has_side_effects=True, vmem_limit_bytes=60 * 2**20
         ),
     )(
-        parents, lengths, page_lists, queries.reshape(4, 2, 16, WIDTH), prompt_latent, pool_latent, value_up
+        parents, lengths, page_lists, queries, prompt_latent.swapaxes(1, 2), pool_latent, value_up
     )
     return result.reshape(32, 4, VDIM)
 

time: 51.1 us -> 48.2 us (0.943); the launches traced: 51 us -> 47.5 us
  Pallas kernels: 47.8 us -> 46.1 us
  local copies, waits for them, and re-layouts: 3.05 us -> 1.39 us
    pallas_call x1, Pallas kernels: 47.8 us -> 46.1 us  [body(): pl.pallas_call(kernel, out_shape=jax.ShapeDtypeStruct((8, 16, VDIM), BF16...]
    reshape x1 -> x0, local copies, waits for them, and re-layouts: 0.99 us -> none  [body(): queries.reshape(4, 2, 16, WIDTH)]
    unnamed x12 -> x1, local copies, waits for them, and re-layouts: 2.06 us -> 1.39 us
where the time goes in v2:
time: 48.2 us; the launch traced here: 47.5 us
  Pallas kernels  46.1 us (96%)
  local copies, waits for them, and re-layouts  1.39 us (3%)
    pallas_call x1, Pallas kernels, body(): pl.pallas_call(kernel, out_shape=jax.ShapeDtypeStruct((8, 16, VDIM), BF16...  46.1 us
    unnamed x1, local copies, waits for them, and re-layouts  1.39 us

profile of v2, /device:TPU:8, one launch (start us, length us, event | category | flops | bytes accessed | tf_op | source)
XLA Modules:
  0.0 47.5 jit_solution(8033466970684468181)
XLA Ops:
  0.0 46.1 %shard_map.73 = bf16[8,16,128]{2,1,0:T(8,128)(2,1)} custom-call(s32[32]{0:T(128)} %parents.1, s32[32]{0:T(128)} %lengths.1, s32[32,64]{1,0:T(8,128)} %page_lists.1, bf16[32,4,576]{2,1,0:T(4,128)(2,1)} %queries.1, bf16[4,576,128]{2,1,0:T(8,128)(2,1)} %bitcast.2, bf16[2,64,576]{2,1,0:T(8,128)(2,1)} %pool.1, bf16[4,512,128]{2,1,0:T(8,128)(2,1)} %value_up.1), custom_call_target="tpu_custom_call" | custom-call | tf_op jit(solution)/shard_map/pallas_call | solution.py:306
  46.1 1.4 %copy.9 = bf16[32,4,128]{2,1,0:T(4,128)(2,1)} copy(bf16[32,4,128]{2,1,0:T(4,128)(2,1)} %bitcast.3) | data formatting | bytes 65536

commit v3 on v2

--- a/solution.py
+++ b/solution.py
@@ -13,7 +13,8 @@
 PAGE = 64
 MAXP = 64
 NZ = 8
-PACK = LAT + 128
+RELATIVE = (4, 3, 5, 2, 6, 1, 7, 0)
+SLOT = {dz: k for k, dz in enumerate(RELATIVE)}
 KEYS = 128
 LOG2E = 1.4426950408889634
 RATE = (VDIM + ROPE) ** -0.5 * LOG2E
@@ -24,29 +25,6 @@
 
 def place(x, y, z, c):
     return ((y % 2) * 4 + x, z * 4 + (y // 2) * 2 + c)
-
-
-def split3(value):
-    first = value.astype(BF16).astype(F32)
-    rest = value - first
-    second = rest.astype(BF16).astype(F32)
-    return first, second, rest - second
-
-
-def pack_stats(peak, total):
-    rows = peak.shape[0]
-    lane = lax.broadcasted_iota(jnp.int32, (rows, 128), 1)
-    out = jnp.zeros((rows, 128), F32)
-    for i, term in enumerate((*split3(peak), *split3(total))):
-        out = jnp.where(lane == i, term, out)
-    return out.astype(BF16)
-
-
-def unpack_stats(stats):
-    stats = stats.astype(F32)
-    peak = stats[:, 0:1] + stats[:, 1:2] + stats[:, 2:3]
-    total = stats[:, 3:4] + stats[:, 4:5] + stats[:, 5:6]
-    return peak, total
 
 
 def merge(parts, stats):
@@ -63,10 +41,11 @@
 
 
 def kernel(
-    parents, lengths, page_lists, queries, prompt, pool, value_up,
+    parents_hbm, lengths_hbm, lists_hbm, queries, prompt, pool, value_up,
     out,
+    parents, lengths, page_lists,
     q_in, q_wide, q_mirror, q_buf, pool_in, keys, v_buf, lists, room, cap, scores, probs,
-    part, stat, rs1, rs1_stat, rs2_src, rs2, out_src,
+    part, stat, rs1, rs1_stat, rs2_src, rs2_stat_src, rs2, rs2_stat, out_src,
     local_sem, key_send, key_recv, core_send, core_recv, swap_send, swap_recv, q_send, q_recv,
     rs1_send, rs1_recv, rs2_send, rs2_recv, out_send, out_recv,
 ):
@@ -89,21 +68,17 @@
     other_core = place(x, y, z, 1 - c)
     mirror = place(x, 3 - y, z, c)
     key_moves = ((1, 0), (0, 1), (1, 1))
-    scatter_moves = ((2, 0), (0, 2), (2, 2))
+    scatter_moves = ((0, 2), (2, 2), (2, 0))
     out_moves = [(dx, dy) for dy in range(2) for dx in range(4) if (dx, dy) != (0, 0)]
 
     def out_place(dx, dy):
         return place((x + dx) % 4, y_hi * 2 + (y_lo + dy) % 2, z, c)
 
-    def out_source(dx, dy):
-        return place((x - dx + 4) % 4, y_hi * 2 + (y_lo + dy) % 2, z, c)
-
     barrier = pltpu.get_barrier_semaphore()
-    senders = [shifted(dx * step, dy * step, -1) for dx, dy in key_moves]
-    senders += [other_core, mirror]
-    senders += [place(x, y, (z + dz) % NZ, c) for dz in range(1, NZ)]
+    senders = [place(x, y, (z + dz) % NZ, c) for dz in RELATIVE[:-1]]
+    senders += [shifted(dx * step, dy * step, -1) for dx, dy in key_moves]
     senders += [shifted(dx, dy) for dx, dy in scatter_moves]
-    senders += [out_source(dx, dy) for dx, dy in out_moves]
+    senders += [mirror, other_core]
     for sender in senders:
         pl.semaphore_signal(barrier, inc=1, device_id=sender, device_id_type=MESH)
 
@@ -113,10 +88,16 @@
     own_pool = pltpu.make_async_copy(pool, pool_in, local_sem.at[2])
     own_prompt = pltpu.make_async_copy(prompt.at[request], keys.at[c, 0, 0], local_sem.at[3])
     own_v = pltpu.make_async_copy(value_up, v_buf, local_sem.at[4])
+    get_parents = pltpu.make_async_copy(parents_hbm, parents, local_sem.at[5])
+    get_lengths = pltpu.make_async_copy(lengths_hbm, lengths, local_sem.at[6])
+    get_lists = pltpu.make_async_copy(lists_hbm, page_lists, local_sem.at[7])
     own_q.start()
     mirror_q.start()
     own_pool.start()
     own_prompt.start()
+    get_parents.start()
+    get_lengths.start()
+    get_lists.start()
     own_v.start()
 
     def packed(i):
@@ -132,7 +113,7 @@
     mirror_q.wait()
     q_mirror[...] = packed(1)
     own_q.wait()
-    q_buf[y_hi, z] = packed(0)
+    q_buf[y_hi, SLOT[0]] = packed(0)
     own_pool.wait()
     flat_pool = pool_in[...].reshape(KEYS, WIDTH)
     keys[c, 0, 1, :LAT] = flat_pool[:, :LAT].T
@@ -150,27 +131,39 @@
         copies.append(copy)
         return copy
 
-    swap = send(q_mirror, q_buf.at[y_hi, z], swap_send, swap_recv, mirror)
+    swap = send(q_mirror, q_buf.at[y_hi, SLOT[0]], swap_send, swap_recv, mirror)
     q_copies = {}
-    far = (4, 3, 5)
-    near = (2, 6, 1, 7)
-    for dz in far + near:
-        q_copies[0, dz] = send(
-            q_buf.at[y_hi, z], q_buf.at[y_hi, z], q_send.at[0, dz], q_recv.at[0, dz],
-            place(x, y, (z + dz) % NZ, c),
+
+    def along_z(group, dz):
+        slot = SLOT[(NZ - dz) % NZ]
+        q_copies[group, slot] = send(
+            q_buf.at[(y_hi + group) % 2, SLOT[0]], q_buf.at[(y_hi + group) % 2, slot],
+            q_send.at[group, slot], q_recv.at[group, slot], place(x, y, (z + dz) % NZ, c),
         )
-    key_copies = []
-    for i, (dx, dy) in enumerate(key_moves):
-        target_request = (x_lo + dx) % 2 * 2 + (y_lo + dy) % 2
-        target = shifted(dx * step, dy * step)
-        key_copies.append((
-            send(prompt.at[target_request], keys.at[c, i + 1, 0], key_send.at[i, 0], key_recv.at[i, 0], target),
-            send(keys.at[c, 0, 1], keys.at[c, i + 1, 1], key_send.at[i, 1], key_recv.at[i, 1], target),
-        ))
+
+    for dz in RELATIVE[:-1]:
+        along_z(0, dz)
+    key_copies = {}
+    for pooled in range(2):
+        for i, (dx, dy) in enumerate(key_moves):
+            target_request = (x_lo + dx) % 2 * 2 + (y_lo + dy) % 2
+            key_copies[pooled, i + 1] = send(
+                keys.at[c, 0, 1] if pooled else prompt.at[target_request], keys.at[c, i + 1, pooled],
+                key_send.at[i, pooled], key_recv.at[i, pooled], shifted(dx * step, dy * step))
+    core_copies = []
+
+    def to_core(kind, pooled):
+        core_copies.append(send(
+            keys.at[c, kind, pooled], keys.at[c, kind, pooled],
+            core_send.at[kind, pooled], core_recv.at[kind, pooled], other_core))
+
     own_prompt.wait()
-    core_copies = [
-        send(keys.at[c, 0], keys.at[c, 0], core_send.at[0], core_recv.at[0], other_core)]
-
+    to_core(0, 0)
+    to_core(0, 1)
+
+    get_parents.wait()
+    get_lengths.wait()
+    get_lists.wait()
     slot = lax.broadcasted_iota(jnp.int32, (4, MAXP), 1)
     for b in range(BEAM):
         parent = parents[request * BEAM + b]
@@ -192,27 +185,23 @@
             cap[:, (cc * 4 + kind) * KEYS : (cc * 4 + kind + 1) * KEYS] = jnp.where(seen, jnp.inf, -jnp.inf)
 
     swap.wait_recv()
-    for dz in near:
-        q_copies[1, dz] = send(
-            q_buf.at[1 - y_hi, z], q_buf.at[1 - y_hi, z], q_send.at[1, dz], q_recv.at[1, dz],
-            place(x, y, (z + dz) % NZ, c),
-        )
-    for dz in far:
-        q_copies[0, dz].wait_recv()
-        source = (z - dz + NZ) % NZ
-        q_copies[1, dz] = send(
-            q_buf.at[y_hi, source], q_buf.at[y_hi, source], q_send.at[1, dz], q_recv.at[1, dz], shifted(0, 2))
-    for i, (prompt_copy, pool_copy) in enumerate(key_copies):
-        prompt_copy.wait_recv()
-        pool_copy.wait_recv()
-        core_copies.append(send(
-            keys.at[c, i + 1], keys.at[c, i + 1], core_send.at[i + 1], core_recv.at[i + 1], other_core))
+    for dz in RELATIVE[1:-1]:
+        along_z(1, dz)
+    for kind in range(1, 4):
+        key_copies[0, kind].wait_recv()
+        to_core(kind, 0)
+    q_copies[0, 0].wait_recv()
+    q_copies[1, 0] = send(
+        q_buf.at[y_hi, 0], q_buf.at[y_hi, 0], q_send.at[1, 0], q_recv.at[1, 0], shifted(0, 2))
+    for kind in range(1, 4):
+        key_copies[1, kind].wait_recv()
+        to_core(kind, 1)
     for copy in core_copies:
         copy.wait_recv()
 
     key_blocks = [(cc, kind, pooled) for pooled in range(2) for cc in range(2) for kind in range(4)]
 
-    rs1_copies = []
+    rs1_copies = {}
 
     def attend(group):
         block = q_buf[group].reshape(KEYS, 2 * LAT + 128)
@@ -242,51 +231,74 @@
             half_rows = slice(half * KEYS, (half + 1) * KEYS)
             stat[group, half] = jnp.where(lane == 0, peak[half_rows], total[half_rows]).T[:8]
 
-    def scatter(i, group, half):
-        dx, dy = scatter_moves[i]
-        rs1_copies.append(send(
-            part.at[group, half], rs1.at[i], rs1_send.at[i, 0], rs1_recv.at[i, 0], shifted(dx, dy)))
-        rs1_copies.append(send(
-            stat.at[group, half], rs1_stat.at[i], rs1_send.at[i, 1], rs1_recv.at[i, 1], shifted(dx, dy)))
-
-    for dz in near:
-        q_copies[0, dz].wait_recv()
+    chunks = (slice(0, 64), slice(64, 128))
+
+    def scatter(i, group, half, chunk):
+        rows = pl.ds(64 * chunk, 64)
+        rs1_copies[i, chunk] = send(
+            part.at[group, half, rows], rs1.at[i, rows],
+            rs1_send.at[i, chunk], rs1_recv.at[i, chunk], shifted(*scatter_moves[i]))
+
+    def scatter_stat(i, group, half):
+        rs1_copies[i, 2] = send(
+            stat.at[group, half], rs1_stat.at[i], rs1_send.at[i, 2], rs1_recv.at[i, 2], shifted(*scatter_moves[i]))
+
+    for slot in range(1, NZ - 1):
+        q_copies[0, slot].wait_recv()
     attend(y_hi)
-    scatter(0, y_hi, 1 - x_hi)
-    for dz in near + far:
-        q_copies[1, dz].wait_recv()
+    scatter_stat(1, y_hi, 1 - x_hi)
+    scatter_stat(0, y_hi, x_hi)
+    for chunk in range(2):
+        scatter(1, y_hi, 1 - x_hi, chunk)
+        scatter(0, y_hi, x_hi, chunk)
+    for slot in range(NZ - 1):
+        q_copies[1, slot].wait_recv()
     attend(1 - y_hi)
-    scatter(2, 1 - y_hi, 1 - x_hi)
-    scatter(1, 1 - y_hi, x_hi)
-
-    for copy in rs1_copies:
-        copy.wait_recv()
+    scatter_stat(2, 1 - y_hi, 1 - x_hi)
+    for chunk in range(2):
+        scatter(2, 1 - y_hi, 1 - x_hi, chunk)
+
+    rs2_copies = []
+    for i in range(3):
+        rs1_copies[i, 2].wait_recv()
     columns = jnp.concatenate([
-        stat[y_hi, x_hi], rs1_stat[0], rs1_stat[1], rs1_stat[2], jnp.zeros((KEYS - 32, KEYS), F32)], axis=0).T
-    peak, total, latent = merge(
-        [part[y_hi, x_hi], rs1[0], rs1[1], rs1[2]],
-        [(columns[:, 8 * i : 8 * i + 1], columns[:, 8 * i + 1 : 8 * i + 2]) for i in range(4)])
-    rs2_src[:, :, :LAT] = latent.astype(BF16).reshape(NZ, 16, LAT)
-    rs2_src[:, :, LAT:] = pack_stats(peak, total).reshape(NZ, 16, 128)
-    rs2_copies = []
-    for dz in far + near:
-        target_z = (z + dz) % NZ
-        rs2_copies.append(send(
-            rs2_src.at[target_z], rs2.at[dz], rs2_send.at[dz], rs2_recv.at[dz], place(x, y, target_z, c)))
-    rs2[0] = rs2_src[z]
+        stat[1 - y_hi, x_hi], rs1_stat[0], rs1_stat[1], rs1_stat[2], jnp.zeros((KEYS - 32, KEYS), F32)], axis=0).T
+    lane = lax.broadcasted_iota(jnp.int32, (64, KEYS), 1)
+    row = lax.broadcasted_iota(jnp.int32, (64, KEYS), 0) % 16
+    for chunk, rows in enumerate(chunks):
+        for i in range(3):
+            rs1_copies[i, chunk].wait_recv()
+        peak, total, latent = merge(
+            [part[1 - y_hi, x_hi, rows], rs1[0, rows], rs1[1, rows], rs1[2, rows]],
+            [(columns[rows, 8 * i : 8 * i + 1], columns[rows, 8 * i + 1 : 8 * i + 2]) for i in range(4)])
+        rs2_src[4 * chunk : 4 * chunk + 4] = latent.astype(BF16).reshape(4, 16, LAT)
+        spread = jnp.where(lane == row, peak, 0.0) + jnp.where(lane == row + 16, total, 0.0)
+        rs2_stat_src[4 * chunk : 4 * chunk + 4] = jnp.sum(spread.reshape(4, 16, KEYS), axis=1, keepdims=True)
+        for slot in range(4 * chunk, 4 * chunk + 4):
+            target = place(x, 3 - y, (z + RELATIVE[slot]) % NZ, c)
+            rs2_copies.append(send(
+                rs2_src.at[slot], rs2.at[slot], rs2_send.at[slot, 0], rs2_recv.at[slot, 0], target))
+            rs2_copies.append(send(
+                rs2_stat_src.at[slot], rs2_stat.at[slot], rs2_send.at[slot, 1], rs2_recv.at[slot, 1], target))
     own_v.wait()
     for copy in rs2_copies:
         copy.wait_recv()
-    blocks = [rs2[i] for i in range(NZ)]
-    peak, total, latent = merge(blocks, [unpack_stats(block[:, LAT:]) for block in blocks])
+    lane = lax.broadcasted_iota(jnp.int32, (16, KEYS), 1)
+    row = lax.broadcasted_iota(jnp.int32, (16, KEYS), 0)
+    stats = []
+    for slot in range(NZ):
+        line = rs2_stat[slot]
+        stats.append((
+            jnp.sum(jnp.where(lane == row, line, 0.0), axis=1, keepdims=True),
+            jnp.sum(jnp.where(lane == row + 16, line, 0.0), axis=1, keepdims=True)))
+    peak, total, latent = merge([rs2[slot] for slot in range(NZ)], stats)
     latent = (latent / total).astype(BF16)
-    row = lax.broadcasted_iota(jnp.int32, (16, VDIM), 0) % 4
     attended = jnp.zeros((16, VDIM), F32)
     for h in range(4):
         product = jnp.dot(latent, v_buf[h], preferred_element_type=F32)
-        attended = jnp.where(row == h, product, attended)
+        attended = jnp.where(row % 4 == h, product, attended)
     out_src[...] = attended.astype(BF16)
-    place_out = request * 2 + x_hi
+    place_out = mirror_request * 2 + x_hi
     out_copies = []
     for i, (dx, dy) in enumerate(out_moves):
         out_copies.append(send(
@@ -300,15 +312,17 @@
 
 def body(queries, prompt_latent, pool_latent, value_up, parents, page_lists, lengths):
     vmem = pl.BlockSpec(memory_space=pltpu.VMEM)
-    smem = pl.BlockSpec(memory_space=pltpu.SMEM)
-    hbm = pl.BlockSpec(memory_space=pl.ANY)
+    hbm = pl.BlockSpec(memory_space=pltpu.HBM)
     dma = pltpu.SemaphoreType.DMA
     result = pl.pallas_call(
         kernel,
         out_shape=jax.ShapeDtypeStruct((8, 16, VDIM), BF16),
-        in_specs=[smem, smem, vmem, hbm, hbm, hbm, hbm],
+        in_specs=[hbm] * 7,
         out_specs=vmem,
         scratch_shapes=[
+            pltpu.SMEM((32,), jnp.int32),
+            pltpu.SMEM((32,), jnp.int32),
+            pltpu.VMEM((32, MAXP), jnp.int32),
             pltpu.VMEM((2, BEAM, 4, WIDTH), BF16),
             pltpu.VMEM((2, 16, 2 * LAT + 128), F32),
             pltpu.VMEM((16, 2 * LAT + 128), BF16),
@@ -325,11 +339,13 @@
             pltpu.VMEM((2, 2, 8, KEYS), F32),
             pltpu.VMEM((3, KEYS, LAT), BF16),
             pltpu.VMEM((3, 8, KEYS), F32),
-            pltpu.VMEM((NZ, 16, PACK), BF16),
-            pltpu.VMEM((NZ, 16, PACK), BF16),
+            pltpu.VMEM((NZ, 16, LAT), BF16),
+            pltpu.VMEM((NZ, 1, KEYS), F32),
+            pltpu.VMEM((NZ, 16, LAT), BF16),
+            pltpu.VMEM((NZ, 1, KEYS), F32),
             pltpu.VMEM((16, VDIM), BF16),
-            dma((5,)), dma((3, 2)), dma((3, 2)), dma((4,)), dma((4,)), dma, dma, dma((2, NZ)), dma((2, NZ)),
-            dma((3, 2)), dma((3, 2)), dma((NZ,)), dma((NZ,)), dma((7,)), dma((7,)),
+            dma((8,)), dma((3, 2)), dma((3, 2)), dma((4, 2)), dma((4, 2)), dma, dma, dma((2, NZ)), dma((2, NZ)),
+            dma((3, 3)), dma((3, 3)), dma((NZ, 2)), dma((NZ, 2)), dma((7,)), dma((7,)),
         ],
         compiler_params=pltpu.CompilerParams(
             collective_id=0, has_side_effects=True, vmem_limit_bytes=60 * 2**20

time: 48.2 us -> 44.2 us (0.917); the launches traced: 47.5 us -> 44 us
  Pallas kernels: 46.1 us -> 42.6 us
    pallas_call x1, Pallas kernels: 46.1 us -> 42.6 us  [body(): pl.pallas_call(kernel, out_shape=jax.ShapeDtypeStruct((8, 16, VDIM), BF16...]
where the time goes in v3:
time: 44.2 us; the launch traced here: 44 us
  Pallas kernels  42.6 us (96%)
  local copies, waits for them, and re-layouts  1.39 us (3%)
    pallas_call x1, Pallas kernels, body(): pl.pallas_call(kernel, out_shape=jax.ShapeDtypeStruct((8, 16, VDIM), BF16...  42.6 us
    unnamed x1, local copies, waits for them, and re-layouts  1.39 us

profile of v3, /device:TPU:8, one launch (start us, length us, event | category | flops | bytes accessed | tf_op | source)
XLA Modules:
  0.0 44.0 jit_solution(1857053916696492849)
XLA Ops:
  0.0 42.6 %shard_map.73 = bf16[8,16,128]{2,1,0:T(8,128)(2,1)} custom-call(s32[32]{0:T(128)} %parents_hbm.1, s32[32]{0:T(128)} %lengths_hbm.1, s32[32,64]{1,0:T(8,128)} %lists_hbm.1, bf16[32,4,576]{2,1,0:T(4,128)(2,1)} %queries.1, bf16[4,576,128]{2,1,0:T(8,128)(2,1)} %bitcast.2, bf16[2,64,576]{2,1,0:T(8,128)(2,1)} %pool.1, bf16[4,512,128]{2,1,0:T(8,128)(2,1)} %value_up.1), custom_call_target="tpu_custom_call" | custom-call | tf_op jit(solution)/shard_map/pallas_call | solution.py:317
  42.6 1.4 %copy.9 = bf16[32,4,128]{2,1,0:T(4,128)(2,1)} copy(bf16[32,4,128]{2,1,0:T(4,128)(2,1)} %bitcast.3) | data formatting | bytes 65536

commit v4 on v3

--- a/solution.py
+++ b/solution.py
@@ -40,14 +40,30 @@
     return peak, total, latent
 
 
+def lines(peak, total):
+    rows = peak.shape[0]
+    lane = lax.broadcasted_iota(jnp.int32, (rows, KEYS), 1)
+    row = lax.broadcasted_iota(jnp.int32, (rows, KEYS), 0) % 16
+    spread = jnp.where(lane == row, peak, 0.0) + jnp.where(lane == row + 16, total, 0.0)
+    return jnp.sum(spread.reshape(rows // 16, 16, KEYS), axis=1, keepdims=True)
+
+
+def from_line(line):
+    lane = lax.broadcasted_iota(jnp.int32, (16, KEYS), 1)
+    row = lax.broadcasted_iota(jnp.int32, (16, KEYS), 0)
+    return (
+        jnp.sum(jnp.where(lane == row, line, 0.0), axis=1, keepdims=True),
+        jnp.sum(jnp.where(lane == row + 16, line, 0.0), axis=1, keepdims=True))
+
+
 def kernel(
     parents_hbm, lengths_hbm, lists_hbm, queries, prompt, pool, value_up,
     out,
     parents, lengths, page_lists,
     q_in, q_wide, q_mirror, q_buf, pool_in, keys, v_buf, lists, room, cap, scores, probs,
-    part, stat, rs1, rs1_stat, rs2_src, rs2_stat_src, rs2, rs2_stat, out_src,
+    part, stat, rs1, rs1_stat, zs, zs_stat_src, zs_stat, rs2_src, rs2_stat_src, rs2, rs2_stat, out_src,
     local_sem, key_send, key_recv, core_send, core_recv, swap_send, swap_recv, q_send, q_recv,
-    rs1_send, rs1_recv, rs2_send, rs2_recv, out_send, out_recv,
+    rs1_send, rs1_recv, zs_send, zs_recv, rs2_send, rs2_recv, out_send, out_recv,
 ):
     seq = lax.axis_index("seq")
     head = lax.axis_index("head")
@@ -68,7 +84,7 @@
     other_core = place(x, y, z, 1 - c)
     mirror = place(x, 3 - y, z, c)
     key_moves = ((1, 0), (0, 1), (1, 1))
-    scatter_moves = ((0, 2), (2, 2), (2, 0))
+    scatter_moves = ((0, 2), (2, 0))
     out_moves = [(dx, dy) for dy in range(2) for dx in range(4) if (dx, dy) != (0, 0)]
 
     def out_place(dx, dy):
@@ -141,25 +157,35 @@
             q_send.at[group, slot], q_recv.at[group, slot], place(x, y, (z + dz) % NZ, c),
         )
 
+    pieces = ((0, slice(0, WIDTH)), (1, slice(0, WIDTH // 2)), (1, slice(WIDTH // 2, WIDTH)))
+    key_copies = {}
+
+    def key_piece(kind, piece):
+        pooled, rows = pieces[piece]
+        dx, dy = key_moves[kind - 1]
+        target_request = (x_lo + dx) % 2 * 2 + (y_lo + dy) % 2
+        key_copies[kind, piece] = send(
+            keys.at[c, 0, 1, rows] if pooled else prompt.at[target_request], keys.at[c, kind, pooled, rows],
+            key_send.at[kind - 1, piece], key_recv.at[kind - 1, piece], shifted(dx * step, dy * step))
+
+    core_copies = []
+
+    def to_core(kind, piece):
+        pooled, rows = pieces[piece]
+        core_copies.append(send(
+            keys.at[c, kind, pooled, rows], keys.at[c, kind, pooled, rows],
+            core_send.at[kind, piece], core_recv.at[kind, piece], other_core))
+
+    for kind in range(1, 4):
+        key_piece(kind, 0)
     for dz in RELATIVE[:-1]:
         along_z(0, dz)
-    key_copies = {}
-    for pooled in range(2):
-        for i, (dx, dy) in enumerate(key_moves):
-            target_request = (x_lo + dx) % 2 * 2 + (y_lo + dy) % 2
-            key_copies[pooled, i + 1] = send(
-                keys.at[c, 0, 1] if pooled else prompt.at[target_request], keys.at[c, i + 1, pooled],
-                key_send.at[i, pooled], key_recv.at[i, pooled], shifted(dx * step, dy * step))
-    core_copies = []
-
-    def to_core(kind, pooled):
-        core_copies.append(send(
-            keys.at[c, kind, pooled], keys.at[c, kind, pooled],
-            core_send.at[kind, pooled], core_recv.at[kind, pooled], other_core))
-
+    for piece in (1, 2):
+        for kind in range(1, 4):
+            key_piece(kind, piece)
     own_prompt.wait()
-    to_core(0, 0)
-    to_core(0, 1)
+    for piece in range(3):
+        to_core(0, piece)
 
     get_parents.wait()
     get_lengths.wait()
@@ -188,14 +214,15 @@
     for dz in RELATIVE[1:-1]:
         along_z(1, dz)
     for kind in range(1, 4):
-        key_copies[0, kind].wait_recv()
+        key_copies[kind, 0].wait_recv()
         to_core(kind, 0)
     q_copies[0, 0].wait_recv()
     q_copies[1, 0] = send(
         q_buf.at[y_hi, 0], q_buf.at[y_hi, 0], q_send.at[1, 0], q_recv.at[1, 0], shifted(0, 2))
-    for kind in range(1, 4):
-        key_copies[1, kind].wait_recv()
-        to_core(kind, 1)
+    for piece in (1, 2):
+        for kind in range(1, 4):
+            key_copies[kind, piece].wait_recv()
+            to_core(kind, piece)
     for copy in core_copies:
         copy.wait_recv()
 
@@ -203,7 +230,7 @@
 
     rs1_copies = {}
 
-    def attend(group):
+    def attend(group, z_first):
         block = q_buf[group].reshape(KEYS, 2 * LAT + 128)
         rotary = block[:, 2 * LAT :]
         lane = lax.broadcasted_iota(jnp.int32, (KEYS, 128), 1)
@@ -230,6 +257,8 @@
         for half in range(2):
             half_rows = slice(half * KEYS, (half + 1) * KEYS)
             stat[group, half] = jnp.where(lane == 0, peak[half_rows], total[half_rows]).T[:8]
+            if z_first:
+                zs_stat_src[half] = lines(peak[half_rows], total[half_rows])
 
     chunks = (slice(0, 64), slice(64, 128))
 
@@ -243,57 +272,63 @@
         rs1_copies[i, 2] = send(
             stat.at[group, half], rs1_stat.at[i], rs1_send.at[i, 2], rs1_recv.at[i, 2], shifted(*scatter_moves[i]))
 
+    zs_copies = []
     for slot in range(1, NZ - 1):
         q_copies[0, slot].wait_recv()
-    attend(y_hi)
-    scatter_stat(1, y_hi, 1 - x_hi)
+    attend(y_hi, True)
     scatter_stat(0, y_hi, x_hi)
-    for chunk in range(2):
-        scatter(1, y_hi, 1 - x_hi, chunk)
-        scatter(0, y_hi, x_hi, chunk)
+    scatter(0, y_hi, x_hi, 0)
+    for slot in range(NZ - 1):
+        target = place(x, y, (z + RELATIVE[slot]) % NZ, c)
+        zs_copies.append(send(
+            part.at[y_hi, 1 - x_hi, pl.ds(16 * slot, 16)], zs.at[slot], zs_send.at[slot, 0], zs_recv.at[slot, 0], target))
+        zs_copies.append(send(
+            zs_stat_src.at[1 - x_hi, slot], zs_stat.at[slot], zs_send.at[slot, 1], zs_recv.at[slot, 1], target))
+    scatter(0, y_hi, x_hi, 1)
     for slot in range(NZ - 1):
         q_copies[1, slot].wait_recv()
-    attend(1 - y_hi)
-    scatter_stat(2, 1 - y_hi, 1 - x_hi)
+    attend(1 - y_hi, False)
+    scatter_stat(1, 1 - y_hi, 1 - x_hi)
     for chunk in range(2):
-        scatter(2, 1 - y_hi, 1 - x_hi, chunk)
+        scatter(1, 1 - y_hi, 1 - x_hi, chunk)
 
     rs2_copies = []
-    for i in range(3):
+
+    def home(slot, target):
+        rs2_copies.append(send(
+            rs2_src.at[slot], rs2.at[slot], rs2_send.at[slot, 0], rs2_recv.at[slot, 0], target))
+        rs2_copies.append(send(
+            rs2_stat_src.at[slot], rs2_stat.at[slot], rs2_send.at[slot, 1], rs2_recv.at[slot, 1], target))
+
+    for i in range(2):
         rs1_copies[i, 2].wait_recv()
     columns = jnp.concatenate([
-        stat[1 - y_hi, x_hi], rs1_stat[0], rs1_stat[1], rs1_stat[2], jnp.zeros((KEYS - 32, KEYS), F32)], axis=0).T
-    lane = lax.broadcasted_iota(jnp.int32, (64, KEYS), 1)
-    row = lax.broadcasted_iota(jnp.int32, (64, KEYS), 0) % 16
+        stat[1 - y_hi, x_hi], rs1_stat[0], rs1_stat[1], jnp.zeros((KEYS - 24, KEYS), F32)], axis=0).T
     for chunk, rows in enumerate(chunks):
-        for i in range(3):
+        for i in range(2):
             rs1_copies[i, chunk].wait_recv()
         peak, total, latent = merge(
-            [part[1 - y_hi, x_hi, rows], rs1[0, rows], rs1[1, rows], rs1[2, rows]],
-            [(columns[rows, 8 * i : 8 * i + 1], columns[rows, 8 * i + 1 : 8 * i + 2]) for i in range(4)])
+            [part[1 - y_hi, x_hi, rows], rs1[0, rows], rs1[1, rows]],
+            [(columns[rows, 8 * i : 8 * i + 1], columns[rows, 8 * i + 1 : 8 * i + 2]) for i in range(3)])
         rs2_src[4 * chunk : 4 * chunk + 4] = latent.astype(BF16).reshape(4, 16, LAT)
-        spread = jnp.where(lane == row, peak, 0.0) + jnp.where(lane == row + 16, total, 0.0)
-        rs2_stat_src[4 * chunk : 4 * chunk + 4] = jnp.sum(spread.reshape(4, 16, KEYS), axis=1, keepdims=True)
+        rs2_stat_src[4 * chunk : 4 * chunk + 4] = lines(peak, total)
         for slot in range(4 * chunk, 4 * chunk + 4):
-            target = place(x, 3 - y, (z + RELATIVE[slot]) % NZ, c)
-            rs2_copies.append(send(
-                rs2_src.at[slot], rs2.at[slot], rs2_send.at[slot, 0], rs2_recv.at[slot, 0], target))
-            rs2_copies.append(send(
-                rs2_stat_src.at[slot], rs2_stat.at[slot], rs2_send.at[slot, 1], rs2_recv.at[slot, 1], target))
+            home(slot, place(x, 3 - y, (z + RELATIVE[slot]) % NZ, c))
+    for copy in zs_copies:
+        copy.wait_recv()
+    peak, total, latent = merge(
+        [part[y_hi, 1 - x_hi, 16 * SLOT[0] :]] + [zs[slot] for slot in range(NZ - 1)],
+        [from_line(zs_stat_src[1 - x_hi, SLOT[0]])] + [from_line(zs_stat[slot]) for slot in range(NZ - 1)])
+    rs2_src[NZ] = latent.astype(BF16)
+    rs2_stat_src[NZ : NZ + 1] = lines(peak, total)
+    home(NZ, place((x + 2) % 4, y_hi * 2 + 1 - y_lo, z, c))
     own_v.wait()
     for copy in rs2_copies:
         copy.wait_recv()
-    lane = lax.broadcasted_iota(jnp.int32, (16, KEYS), 1)
-    row = lax.broadcasted_iota(jnp.int32, (16, KEYS), 0)
-    stats = []
-    for slot in range(NZ):
-        line = rs2_stat[slot]
-        stats.append((
-            jnp.sum(jnp.where(lane == row, line, 0.0), axis=1, keepdims=True),
-            jnp.sum(jnp.where(lane == row + 16, line, 0.0), axis=1, keepdims=True)))
-    peak, total, latent = merge([rs2[slot] for slot in range(NZ)], stats)
+    peak, total, latent = merge([rs2[slot] for slot in range(NZ + 1)], [from_line(rs2_stat[slot]) for slot in range(NZ + 1)])
     latent = (latent / total).astype(BF16)
     attended = jnp.zeros((16, VDIM), F32)
+    row = lax.broadcasted_iota(jnp.int32, (16, VDIM), 0)
     for h in range(4):
         product = jnp.dot(latent, v_buf[h], preferred_element_type=F32)
         attended = jnp.where(row % 4 == h, product, attended)
@@ -313,10 +348,11 @@
 def body(queries, prompt_latent, pool_latent, value_up, parents, page_lists, lengths):
     vmem = pl.BlockSpec(memory_space=pltpu.VMEM)
     hbm = pl.BlockSpec(memory_space=pltpu.HBM)
+    operands = (parents, lengths, page_lists, queries, prompt_latent.swapaxes(1, 2), pool_latent, value_up)
     dma = pltpu.SemaphoreType.DMA
     result = pl.pallas_call(
         kernel,
-        out_shape=jax.ShapeDtypeStruct((8, 16, VDIM), BF16),
+        out_shape=pltpu.VMEM((8, 16, VDIM), BF16),
         in_specs=[hbm] * 7,
         out_specs=vmem,
         scratch_shapes=[
@@ -337,21 +373,24 @@
             pltpu.VMEM((2 * KEYS, 16 * KEYS), BF16),
             pltpu.VMEM((2, 2, KEYS, LAT), BF16),
             pltpu.VMEM((2, 2, 8, KEYS), F32),
-            pltpu.VMEM((3, KEYS, LAT), BF16),
-            pltpu.VMEM((3, 8, KEYS), F32),
-            pltpu.VMEM((NZ, 16, LAT), BF16),
-            pltpu.VMEM((NZ, 1, KEYS), F32),
-            pltpu.VMEM((NZ, 16, LAT), BF16),
-            pltpu.VMEM((NZ, 1, KEYS), F32),
+            pltpu.VMEM((2, KEYS, LAT), BF16),
+            pltpu.VMEM((2, 8, KEYS), F32),
+            pltpu.VMEM((NZ - 1, 16, LAT), BF16),
+            pltpu.VMEM((2, NZ, 1, KEYS), F32),
+            pltpu.VMEM((NZ - 1, 1, KEYS), F32),
+            pltpu.VMEM((NZ + 1, 16, LAT), BF16),
+            pltpu.VMEM((NZ + 1, 1, KEYS), F32),
+            pltpu.VMEM((NZ + 1, 16, LAT), BF16),
+            pltpu.VMEM((NZ + 1, 1, KEYS), F32),
             pltpu.VMEM((16, VDIM), BF16),
-            dma((8,)), dma((3, 2)), dma((3, 2)), dma((4, 2)), dma((4, 2)), dma, dma, dma((2, NZ)), dma((2, NZ)),
-            dma((3, 3)), dma((3, 3)), dma((NZ, 2)), dma((NZ, 2)), dma((7,)), dma((7,)),
+            dma((8,)), dma((3, 3)), dma((3, 3)), dma((4, 3)), dma((4, 3)), dma, dma, dma((2, NZ)), dma((2, NZ)),
+            dma((2, 3)), dma((2, 3)), dma((NZ - 1, 2)), dma((NZ - 1, 2)), dma((NZ + 1, 2)), dma((NZ + 1, 2)), dma((7,)), dma((7,)),
         ],
         compiler_params=pltpu.CompilerParams(
-            collective_id=0, has_side_effects=True, vmem_limit_bytes=60 * 2**20
+            collective_id=0, has_side_effects=True, vmem_limit_bytes=48 * 2**20
         ),
     )(
-        parents, lengths, page_lists, queries, prompt_latent.swapaxes(1, 2), pool_latent, value_up
+        *[pltpu.with_memory_space_constraint(operand, pltpu.HBM) for operand in operands]
     )
     return result.reshape(32, 4, VDIM)
 

time: 44.2 us -> 41.6 us (0.941)
  Pallas kernels: 42.6 us -> 40.7 us
  local copies, waits for them, and re-layouts: 1.39 us -> 0.62 us
    pallas_call x1, Pallas kernels: 42.6 us -> 40.7 us  [body(): pl.pallas_call(kernel, out_shape=pltpu.VMEM((8, 16, VDIM), BF16), in_spec...]
    unnamed x1, local copies, waits for them, and re-layouts: 1.39 us -> 0.62 us
where the time goes in v4:
time: 41.6 us; the launch traced here: 41.3 us
  Pallas kernels  40.7 us (98%)
  local copies, waits for them, and re-layouts  0.62 us (1%)
    pallas_call x1, Pallas kernels, body(): pl.pallas_call(kernel, out_shape=pltpu.VMEM((8, 16, VDIM), BF16), in_spec...  40.7 us

profile of v4, /device:TPU:8, one launch (start us, length us, event | category | flops | bytes accessed | tf_op | source)
XLA Modules:
  0.0 41.3 jit_solution(14121733636668800205)
XLA Ops:
  0.0 40.7 %shard_map.73 = bf16[8,16,128]{2,1,0:T(8,128)(2,1)S(1)} custom-call(s32[32]{0:T(128)} %parents_hbm.1, s32[32]{0:T(128)} %lengths_hbm.1, s32[32,64]{1,0:T(8,128)} %lists_hbm.1, bf16[32,4,576]{2,1,0:T(4,128)(2,1)} %queries.1, bf16[4,576,128]{2,1,0:T(8,128)(2,1)} %bitcast.3, bf16[2,64,576]{2,1,0:T(8,128)(2,1)} %pool.1, bf16[4,512,128]{2,1,0:T(8,128)(2,1)} %value_up.1), custom_call_target="tpu_custom_call" | custom-call | tf_op jit(solution)/shard_map/pallas_call | solution.py:353
  40.7 0.6 %copy.9 = bf16[32,4,128]{2,1,0:T(4,128)(2,1)} copy(bf16[32,4,128]{2,1,0:T(4,128)(2,1)S(1)} %bitcast.2) | data formatting | bytes 65536

commit v5 on v4

--- a/solution.py
+++ b/solution.py
@@ -14,10 +14,13 @@
 MAXP = 64
 NZ = 8
 RELATIVE = (4, 3, 5, 2, 6, 1, 7, 0)
+CHUNKS = 2
+CHUNK = 128 // CHUNKS
 SLOT = {dz: k for k, dz in enumerate(RELATIVE)}
 KEYS = 128
 LOG2E = 1.4426950408889634
 RATE = (VDIM + ROPE) ** -0.5 * LOG2E
+LOWEST = -3.0e38
 MESH = pl.DeviceIdType.MESH
 F32 = jnp.float32
 BF16 = jnp.bfloat16
@@ -91,7 +94,7 @@
         return place((x + dx) % 4, y_hi * 2 + (y_lo + dy) % 2, z, c)
 
     barrier = pltpu.get_barrier_semaphore()
-    senders = [place(x, y, (z + dz) % NZ, c) for dz in RELATIVE[:-1]]
+    senders = [place(x, y, (z + dz) % NZ, c) for dz in (2, 6, 1, 7)]
     senders += [shifted(dx * step, dy * step, -1) for dx, dy in key_moves]
     senders += [shifted(dx, dy) for dx, dy in scatter_moves]
     senders += [mirror, other_core]
@@ -150,13 +153,28 @@
     swap = send(q_mirror, q_buf.at[y_hi, SLOT[0]], swap_send, swap_recv, mirror)
     q_copies = {}
 
-    def along_z(group, dz):
-        slot = SLOT[(NZ - dz) % NZ]
+    def along_z(group, source, dz, slot):
+        side = (y_hi + group) % 2
         q_copies[group, slot] = send(
-            q_buf.at[(y_hi + group) % 2, SLOT[0]], q_buf.at[(y_hi + group) % 2, slot],
-            q_send.at[group, slot], q_recv.at[group, slot], place(x, y, (z + dz) % NZ, c),
-        )
-
+            q_buf.at[side, source], q_buf.at[side, slot],
+            q_send.at[group, slot], q_recv.at[group, slot], place(x, y, (z + dz + NZ) % NZ, c))
+
+    def first_step(group):
+        for dz in (2, 6, 1, 7):
+            along_z(group, SLOT[0], dz, SLOT[NZ - dz])
+
+    def second_step(group):
+        q_copies[group, SLOT[6]].wait_recv()
+        q_copies[group, SLOT[2]].wait_recv()
+        along_z(group, SLOT[6] + c * (SLOT[2] - SLOT[6]), 2 * step, SLOT[4])
+        along_z(group, SLOT[6], 1, SLOT[5])
+        along_z(group, SLOT[2], -1, SLOT[3])
+
+    def wait_queries(group):
+        for dz in (1, 7, 3, 5, 4):
+            q_copies[group, SLOT[dz]].wait_recv()
+
+    first_step(0)
     pieces = ((0, slice(0, WIDTH)), (1, slice(0, WIDTH // 2)), (1, slice(WIDTH // 2, WIDTH)))
     key_copies = {}
 
@@ -168,18 +186,20 @@
             keys.at[c, 0, 1, rows] if pooled else prompt.at[target_request], keys.at[c, kind, pooled, rows],
             key_send.at[kind - 1, piece], key_recv.at[kind - 1, piece], shifted(dx * step, dy * step))
 
-    core_copies = []
+    core_copies = {}
 
     def to_core(kind, piece):
         pooled, rows = pieces[piece]
-        core_copies.append(send(
+        core_copies[kind, piece] = send(
             keys.at[c, kind, pooled, rows], keys.at[c, kind, pooled, rows],
-            core_send.at[kind, piece], core_recv.at[kind, piece], other_core))
+            core_send.at[kind, piece], core_recv.at[kind, piece], other_core)
+
+    def wait_core(piece):
+        for kind in range(4):
+            core_copies[kind, piece].wait_recv()
 
     for kind in range(1, 4):
         key_piece(kind, 0)
-    for dz in RELATIVE[:-1]:
-        along_z(0, dz)
     for piece in (1, 2):
         for kind in range(1, 4):
             key_piece(kind, piece)
@@ -211,26 +231,17 @@
             cap[:, (cc * 4 + kind) * KEYS : (cc * 4 + kind + 1) * KEYS] = jnp.where(seen, jnp.inf, -jnp.inf)
 
     swap.wait_recv()
-    for dz in RELATIVE[1:-1]:
-        along_z(1, dz)
+    first_step(1)
+    second_step(0)
     for kind in range(1, 4):
         key_copies[kind, 0].wait_recv()
         to_core(kind, 0)
-    q_copies[0, 0].wait_recv()
-    q_copies[1, 0] = send(
-        q_buf.at[y_hi, 0], q_buf.at[y_hi, 0], q_send.at[1, 0], q_recv.at[1, 0], shifted(0, 2))
-    for piece in (1, 2):
-        for kind in range(1, 4):
-            key_copies[kind, piece].wait_recv()
-            to_core(kind, piece)
-    for copy in core_copies:
-        copy.wait_recv()
-
-    key_blocks = [(cc, kind, pooled) for pooled in range(2) for cc in range(2) for kind in range(4)]
-
-    rs1_copies = {}
-
-    def attend(group, z_first):
+    second_step(1)
+    for kind in range(1, 4):
+        key_copies[kind, 1].wait_recv()
+        to_core(kind, 1)
+
+    def attend(group, pooled):
         block = q_buf[group].reshape(KEYS, 2 * LAT + 128)
         rotary = block[:, 2 * LAT :]
         lane = lax.broadcasted_iota(jnp.int32, (KEYS, 128), 1)
@@ -238,59 +249,72 @@
             jnp.concatenate([block[:, :LAT], jnp.where(lane < ROPE, rotary, 0)], axis=1),
             jnp.concatenate([block[:, LAT : 2 * LAT], jnp.where(lane < ROPE, 0, rotary)], axis=1),
         ], axis=0)
-        for pair in range(8):
-            columns = jnp.concatenate([keys[k] for k in key_blocks[2 * pair : 2 * pair + 2]], axis=1)
+        for pair in range(4):
+            cc, kind = pair // 2, pair % 2 * 2
+            columns = jnp.concatenate([keys[cc, kind, pooled], keys[cc, kind + 1, pooled]], axis=1)
             columns = jnp.concatenate([columns, columns[LAT:]], axis=0)
             raw = jnp.dot(rows, columns, preferred_element_type=F32)
-            if pair >= 4:
-                limit = cap[:, (2 * pair - 8) * KEYS : (2 * pair - 6) * KEYS].reshape(2, 1, 16, 2 * KEYS)
+            if pooled:
+                limit = cap[:, 2 * pair * KEYS : 2 * (pair + 1) * KEYS].reshape(2, 1, 16, 2 * KEYS)
                 raw = jnp.minimum(raw.reshape(2, NZ, 16, 2 * KEYS), limit).reshape(2 * KEYS, 2 * KEYS)
             scores[:, 2 * pair * KEYS : 2 * (pair + 1) * KEYS] = raw
         peak = jnp.max(scores[...], axis=1, keepdims=True)
+        if pooled:
+            peak = jnp.maximum(peak, LOWEST)
         weights = jnp.exp2((scores[...] - peak) * RATE)
         total = jnp.sum(weights, axis=1, keepdims=True)
         probs[...] = weights.astype(BF16)
-        values = jnp.concatenate([keys[cc, kind, pooled, :LAT] for cc, kind, pooled in key_blocks], axis=1)
+        values = jnp.concatenate([keys[cc, kind, pooled, :LAT] for cc in range(2) for kind in range(4)], axis=1)
         latent = lax.dot_general(
             probs[...], values, (((1,), (1,)), ((), ())), preferred_element_type=F32)
-        part[group] = latent.astype(BF16).reshape(2, KEYS, LAT)
+        return peak, total, latent
+
+    def finish(group, first, z_first):
+        peak1, total1, latent1 = first
+        peak2, total2, latent2 = attend(group, 1)
+        peak = jnp.maximum(peak1, peak2)
+        keep1 = jnp.exp2((peak1 - peak) * RATE)
+        keep2 = jnp.exp2((peak2 - peak) * RATE)
+        total = total1 * keep1 + total2 * keep2
+        part[group] = (latent1 * keep1 + latent2 * keep2).astype(BF16).reshape(2, KEYS, LAT)
+        lane = lax.broadcasted_iota(jnp.int32, (KEYS, 128), 1)
         for half in range(2):
             half_rows = slice(half * KEYS, (half + 1) * KEYS)
             stat[group, half] = jnp.where(lane == 0, peak[half_rows], total[half_rows]).T[:8]
             if z_first:
                 zs_stat_src[half] = lines(peak[half_rows], total[half_rows])
 
-    chunks = (slice(0, 64), slice(64, 128))
-
-    def scatter(i, group, half, chunk):
-        rows = pl.ds(64 * chunk, 64)
-        rs1_copies[i, chunk] = send(
-            part.at[group, half, rows], rs1.at[i, rows],
-            rs1_send.at[i, chunk], rs1_recv.at[i, chunk], shifted(*scatter_moves[i]))
-
-    def scatter_stat(i, group, half):
-        rs1_copies[i, 2] = send(
-            stat.at[group, half], rs1_stat.at[i], rs1_send.at[i, 2], rs1_recv.at[i, 2], shifted(*scatter_moves[i]))
-
+    def scatter(i, group, half):
+        target = shifted(*scatter_moves[i])
+        rs1_copies[i, CHUNKS] = send(
+            stat.at[group, half], rs1_stat.at[i], rs1_send.at[i, CHUNKS], rs1_recv.at[i, CHUNKS], target)
+        for chunk in range(CHUNKS):
+            rows = pl.ds(CHUNK * chunk, CHUNK)
+            rs1_copies[i, chunk] = send(
+                part.at[group, half, rows], rs1.at[i, rows], rs1_send.at[i, chunk], rs1_recv.at[i, chunk], target)
+
+    rs1_copies = {}
     zs_copies = []
-    for slot in range(1, NZ - 1):
-        q_copies[0, slot].wait_recv()
-    attend(y_hi, True)
-    scatter_stat(0, y_hi, x_hi)
-    scatter(0, y_hi, x_hi, 0)
+    wait_queries(0)
+    wait_core(0)
+    prompt_a = attend(y_hi, 0)
+    for kind in range(1, 4):
+        key_copies[kind, 2].wait_recv()
+        to_core(kind, 2)
+    wait_queries(1)
+    prompt_b = attend(1 - y_hi, 0)
+    wait_core(1)
+    wait_core(2)
+    finish(y_hi, prompt_a, True)
     for slot in range(NZ - 1):
         target = place(x, y, (z + RELATIVE[slot]) % NZ, c)
         zs_copies.append(send(
             part.at[y_hi, 1 - x_hi, pl.ds(16 * slot, 16)], zs.at[slot], zs_send.at[slot, 0], zs_recv.at[slot, 0], target))
         zs_copies.append(send(
             zs_stat_src.at[1 - x_hi, slot], zs_stat.at[slot], zs_send.at[slot, 1], zs_recv.at[slot, 1], target))
-    scatter(0, y_hi, x_hi, 1)
-    for slot in range(NZ - 1):
-        q_copies[1, slot].wait_recv()
-    attend(1 - y_hi, False)
-    scatter_stat(1, 1 - y_hi, 1 - x_hi)
-    for chunk in range(2):
-        scatter(1, 1 - y_hi, 1 - x_hi, chunk)
+    scatter(0, y_hi, x_hi)
+    finish(1 - y_hi, prompt_b, False)
+    scatter(1, 1 - y_hi, 1 - x_hi)
 
     rs2_copies = []
 
@@ -301,18 +325,20 @@
             rs2_stat_src.at[slot], rs2_stat.at[slot], rs2_send.at[slot, 1], rs2_recv.at[slot, 1], target))
 
     for i in range(2):
-        rs1_copies[i, 2].wait_recv()
+        rs1_copies[i, CHUNKS].wait_recv()
     columns = jnp.concatenate([
         stat[1 - y_hi, x_hi], rs1_stat[0], rs1_stat[1], jnp.zeros((KEYS - 24, KEYS), F32)], axis=0).T
-    for chunk, rows in enumerate(chunks):
+    per = CHUNK // 16
+    for chunk in range(CHUNKS):
+        rows = slice(chunk * CHUNK, (chunk + 1) * CHUNK)
         for i in range(2):
             rs1_copies[i, chunk].wait_recv()
         peak, total, latent = merge(
             [part[1 - y_hi, x_hi, rows], rs1[0, rows], rs1[1, rows]],
             [(columns[rows, 8 * i : 8 * i + 1], columns[rows, 8 * i + 1 : 8 * i + 2]) for i in range(3)])
-        rs2_src[4 * chunk : 4 * chunk + 4] = latent.astype(BF16).reshape(4, 16, LAT)
-        rs2_stat_src[4 * chunk : 4 * chunk + 4] = lines(peak, total)
-        for slot in range(4 * chunk, 4 * chunk + 4):
+        rs2_src[per * chunk : per * chunk + per] = latent.astype(BF16).reshape(per, 16, LAT)
+        rs2_stat_src[per * chunk : per * chunk + per] = lines(peak, total)
+        for slot in range(per * chunk, per * chunk + per):
             home(slot, place(x, 3 - y, (z + RELATIVE[slot]) % NZ, c))
     for copy in zs_copies:
         copy.wait_recv()
@@ -369,8 +395,8 @@
             pltpu.VMEM((4 * BEAM, MAXP), jnp.int32),
             pltpu.VMEM((4 * BEAM, MAXP), jnp.int32),
             pltpu.VMEM((4 * BEAM, 8 * KEYS), F32),
-            pltpu.VMEM((2 * KEYS, 16 * KEYS), F32),
-            pltpu.VMEM((2 * KEYS, 16 * KEYS), BF16),
+            pltpu.VMEM((2 * KEYS, 8 * KEYS), F32),
+            pltpu.VMEM((2 * KEYS, 8 * KEYS), BF16),
             pltpu.VMEM((2, 2, KEYS, LAT), BF16),
             pltpu.VMEM((2, 2, 8, KEYS), F32),
             pltpu.VMEM((2, KEYS, LAT), BF16),
@@ -384,7 +410,7 @@
             pltpu.VMEM((NZ + 1, 1, KEYS), F32),
             pltpu.VMEM((16, VDIM), BF16),
             dma((8,)), dma((3, 3)), dma((3, 3)), dma((4, 3)), dma((4, 3)), dma, dma, dma((2, NZ)), dma((2, NZ)),
-            dma((2, 3)), dma((2, 3)), dma((NZ - 1, 2)), dma((NZ - 1, 2)), dma((NZ + 1, 2)), dma((NZ + 1, 2)), dma((7,)), dma((7,)),
+            dma((2, CHUNKS + 1)), dma((2, CHUNKS + 1)), dma((NZ - 1, 2)), dma((NZ - 1, 2)), dma((NZ + 1, 2)), dma((NZ + 1, 2)), dma((7,)), dma((7,)),
         ],
         compiler_params=pltpu.CompilerParams(
             collective_id=0, has_side_effects=True, vmem_limit_bytes=48 * 2**20

time: 41.6 us -> 41.5 us (level)
  no operation moved by 1% of the time
where the time goes in v5:
time: 41.5 us
  Pallas kernels  40.8 us (98%)
  local copies, waits for them, and re-layouts  0.62 us (1%)
    pallas_call x1, Pallas kernels, body(): pl.pallas_call(kernel, out_shape=pltpu.VMEM((8, 16, VDIM), BF16), in_spec...  40.8 us

profile of v5, /device:TPU:8, one launch (start us, length us, event | category | flops | bytes accessed | tf_op | source)
XLA Modules:
  0.0 41.5 jit_solution(17104980298397458192)
XLA Ops:
  0.0 40.8 %shard_map.73 = bf16[8,16,128]{2,1,0:T(8,128)(2,1)S(1)} custom-call(s32[32]{0:T(128)} %parents_hbm.1, s32[32]{0:T(128)} %lengths_hbm.1, s32[32,64]{1,0:T(8,128)} %lists_hbm.1, bf16[32,4,576]{2,1,0:T(4,128)(2,1)} %queries.1, bf16[4,576,128]{2,1,0:T(8,128)(2,1)} %bitcast.3, bf16[2,64,576]{2,1,0:T(8,128)(2,1)} %pool.1, bf16[4,512,128]{2,1,0:T(8,128)(2,1)} %value_up.1), custom_call_target="tpu_custom_call" | custom-call | tf_op jit(solution)/shard_map/pallas_call | solution.py:379
  40.8 0.6 %copy.9 = bf16[32,4,128]{2,1,0:T(4,128)(2,1)} copy(bf16[32,4,128]{2,1,0:T(4,128)(2,1)S(1)} %bitcast.2) | data formatting | bytes 65536

commit v6 on v0

v6 whole, which is shorter than its diff:
```python
import jax
import jax.numpy as jnp
from jax import lax
from jax.experimental import pallas as pl
from jax.experimental.pallas import tpu as pltpu
from jax.sharding import PartitionSpec as P

LAT = 512
ROPE = 64
WIDTH = LAT + ROPE
VDIM = 128
BEAM = 8
PAGE = 64
MAXP = 64
NZ = 8
RELATIVE = (4, 3, 5, 2, 6, 1, 7, 0)
BLOCK = 32
ROWS = 256
SLOT = {dz: k for k, dz in enumerate(RELATIVE)}
KEYS = 128
LOG2E = 1.4426950408889634
RATE = (VDIM + ROPE) ** -0.5 * LOG2E
LOWEST = -3.0e38
MESH = pl.DeviceIdType.MESH
F32 = jnp.float32
BF16 = jnp.bfloat16


def place(x, y, z, c):
    return ((y % 2) * 4 + x, z * 4 + (y // 2) * 2 + c)


def merge(parts, stats):
    peak = stats[0][0]
    for other, _ in stats[1:]:
        peak = jnp.maximum(peak, other)
    total = jnp.zeros_like(peak)
    latent = jnp.zeros((peak.shape[0], LAT), F32)
    for part, (part_peak, part_total) in zip(parts, stats):
        keep = jnp.exp2((part_peak - peak) * RATE)
        total = total + part_total * keep
        latent = latent + part[:, :LAT].astype(F32) * keep
    return peak, total, latent


def lines(peak, total):
    rows = peak.shape[0]
    lane = lax.broadcasted_iota(jnp.int32, (rows, KEYS), 1)
    row = lax.broadcasted_iota(jnp.int32, (rows, KEYS), 0) % BLOCK
    spread = jnp.where(lane == row, peak, 0.0) + jnp.where(lane == row + BLOCK, total, 0.0)
    return jnp.sum(spread.reshape(rows // BLOCK, BLOCK, KEYS), axis=1, keepdims=True)


def from_line(line):
    lane = lax.broadcasted_iota(jnp.int32, (BLOCK, KEYS), 1)
    row = lax.broadcasted_iota(jnp.int32, (BLOCK, KEYS), 0)
    return (
        jnp.sum(jnp.where(lane == row, line, 0.0), axis=1, keepdims=True),
        jnp.sum(jnp.where(lane == row + BLOCK, line, 0.0), axis=1, keepdims=True))


def kernel(
    parents_hbm, lengths_hbm, lists_hbm, queries, prompt, pool, value_up,
    out,
    parents, lengths, page_lists,
    q_in, q_wide, q_mirror, q_own, q_buf, pool_in, pool_flat, keys, v_buf, lists, room, cap, scores, probs,
    part, stat, rs1, rs1_stat, zs, zs_stat_src, zs_stat, rs2_src, rs2_stat_src, rs2, rs2_stat, out_src,
    local_sem, key_send, key_recv, swap_send, swap_recv, q_send, q_recv, next_send, next_recv, v_send, v_recv,
    rs1_send, rs1_recv, zs_send, zs_recv, rs2_send, rs2_recv, out_send, out_recv,
):
    seq = lax.axis_index("seq")
    head = lax.axis_index("head")
    x = seq % 4
    y_lo = seq // 4
    c = head % 2
    y_hi = (head // 2) % 2
    z = head // 4
    y = y_hi * 2 + y_lo
    x_hi = x // 2
    x_lo = x % 2
    request = x_lo * 2 + y_lo
    mirror_request = x_lo * 2 + 1 - y_lo

    def shifted(dx, dy, core=1):
        return place((x + dx + 4) % 4, (y + dy + 4) % 4, z, core)

    def up(dz, core=1):
        return place(x, y, (z + dz + NZ) % NZ, core)

    worker = place(x, y, z, 1)
    key_moves = ((0, 0), (1, 0), (0, 1), (1, 1))
    scatter_moves = ((0, 2), (2, 0))
    out_moves = [(dx, dy) for dy in range(2) for dx in range(4)]

    def out_place(dx, dy, core):
        return place((x + dx) % 4, y_hi * 2 + (y_lo + dy) % 2, z, core)

    barrier = pltpu.get_barrier_semaphore()

    @pl.when(c == 1)
    def _():
        senders = [up(dz, core) for core in range(2) for dz in (2, 6, 1, 7)]
        senders += [
            shifted(-dx * (1 - 2 * core), -dy * (1 - 2 * core), core) for core in range(2) for dx, dy in key_moves[1:]]
        senders += [place(x, 3 - y, z, core) for core in range(2)]
        senders += [shifted(dx, dy) for dx, dy in scatter_moves]
        senders += [place(x, y, z, 0)]
        for sender in senders:
            pl.semaphore_signal(barrier, inc=1, device_id=sender, device_id_type=MESH)

    own_q = pltpu.make_async_copy(queries.at[pl.ds(request * BEAM, BEAM)], q_in.at[0], local_sem.at[0])
    mirror_q = pltpu.make_async_copy(queries.at[pl.ds(mirror_request * BEAM, BEAM)], q_in.at[1], local_sem.at[1])
    own_pool = pltpu.make_async_copy(pool, pool_in, local_sem.at[2])
    own_prompt = pltpu.make_async_copy(prompt.at[request], keys.at[1, 0, 0], local_sem.at[3])
    own_v = pltpu.make_async_copy(value_up, v_buf.at[1], local_sem.at[4])
    get_parents = pltpu.make_async_copy(parents_hbm, parents, local_sem.at[5])
    get_lengths = pltpu.make_async_copy(lengths_hbm, lengths, local_sem.at[6])
    get_lists = pltpu.make_async_copy(lists_hbm, page_lists, local_sem.at[7])
    own_q.start()
    mirror_q.start()
    own_pool.start()

    @pl.when(c == 1)
    def _():
        own_prompt.start()
        get_parents.start()
        get_lengths.start()
        get_lists.start()
        own_v.start()

    def packed(i):
        for b in range(BEAM):
            block = q_in[i, b].astype(F32)
            half, start = b // 4, b % 4 * 4
            q_wide[i, start : start + 4, half * LAT : (half + 1) * LAT] = block[:, :LAT]
            if half:
                rotary = jnp.concatenate([q_in[i, b - 4].astype(F32)[:, LAT:], block[:, LAT:]], axis=1)
                q_wide[i, start : start + 4, 2 * LAT :] = rotary
        return q_wide[i].astype(BF16)

    mirror_q.wait()
    q_mirror[...] = packed(1)
    own_q.wait()
    q_own[...] = packed(0)
    own_pool.wait()
    flat_pool = pool_in[...].reshape(KEYS, WIDTH)
    pool_flat[:LAT] = flat_pool[:, :LAT].T
    pool_flat[LAT:] = flat_pool[:, LAT:].T

    @pl.when(c == 1)
    def _():
        q_buf[y_hi, SLOT[0], 1] = q_own[...]
        keys[1, 0, 1] = pool_flat[...]
        pl.semaphore_wait(barrier, 10)

    @pl.when(c == 0)
    def _():
        pl.semaphore_wait(barrier, 9)

    copies = []

    def describe(src, dst, send_sem, recv_sem, target):
        return pltpu.make_async_remote_copy(
            src_ref=src, dst_ref=dst, send_sem=send_sem, recv_sem=recv_sem, device_id=target, device_id_type=MESH)

    def send(*what):
        copy = describe(*what)
        copy.start()
        copies.append(copy)
        return copy

    step = 1 - 2 * c
    send(q_mirror, q_buf.at[y_hi, SLOT[0], c], swap_send, swap_recv.at[c], place(x, 3 - y, z, 1))
    for i, dz in enumerate((2, 6, 1, 7)):
        slot = SLOT[NZ - dz]
        send(q_own, q_buf.at[y_hi, slot, c], q_send.at[i], q_recv.at[c, slot], up(dz))
    pieces = ((0, slice(0, WIDTH)), (1, slice(0, WIDTH // 2)), (1, slice(WIDTH // 2, WIDTH)))

    def key_piece(kind, piece, target):
        pooled, rows = pieces[piece]
        dx, dy = key_moves[kind]
        target_request = (x_lo + dx) % 2 * 2 + (y_lo + dy) % 2
        return describe(
            pool_flat.at[rows] if pooled else prompt.at[target_request], keys.at[c, kind, pooled, rows],
            key_send.at[kind, piece], key_recv.at[c, kind, piece], target)

    for piece in range(3):
        for kind in (3, 1, 2):
            dx, dy = key_moves[kind]
            copy = key_piece(kind, piece, shifted(dx * step, dy * step))
            copy.start()
            copies.append(copy)

    @pl.when(c == 0)
    def _():
        mine = [describe(q_own, q_buf.at[y_hi, SLOT[0], 0], q_send.at[4], q_recv.at[0, SLOT[0]], worker)]
        mine += [key_piece(0, piece, worker) for piece in range(3)]
        mine += [describe(value_up, v_buf.at[0], v_send, v_recv, worker)]
        for copy in mine:
            copy.start()
        for i in range(8):
            describe(out_src.at[0], out.at[0], v_send, out_recv.at[i], worker).wait_recv()
        for copy in mine:
            copy.wait_send()

    @pl.when(c == 1)
    def _():
        work = []

        def post(*what):
            copy = describe(*what)
            copy.start()
            work.append(copy)
            return copy

        def arrived(dst, recv_sem):
            describe(dst, dst, v_send, recv_sem, place(x, y, z, 0)).wait_recv()

        def along_z(group, source, dz, slot):
            side = (y_hi + group) % 2
            post(
                q_buf.at[side, source], q_buf.at[side, slot],
                next_send.at[group, slot], next_recv.at[group, slot], up(dz))

        def await_slot(group, slot):
            side = (y_hi + group) % 2
            if group == 0 and slot not in (SLOT[3], SLOT[4], SLOT[5]):
                for core in range(2):
                    if core == 0 or slot != SLOT[0]:
                        arrived(q_buf.at[side, slot, core], q_recv.at[core, slot])
            else:
                arrived(q_buf.at[side, slot], next_recv.at[group, slot])

        def second_step(group):
            await_slot(group, SLOT[6])
            await_slot(group, SLOT[2])
            if group == 0:
                along_z(group, SLOT[6], 2, SLOT[4])
            else:
                along_z(group, SLOT[2], -2, SLOT[4])
            along_z(group, SLOT[6], 1, SLOT[5])
            along_z(group, SLOT[2], -1, SLOT[3])

        def await_keys(piece, own):
            pooled, rows = pieces[piece]
            for core in range(2):
                for kind in range(4):
                    if (kind == 0) == own and (core == 0 or kind > 0):
                        arrived(keys.at[core, kind, pooled, rows], key_recv.at[core, kind, piece])

        for core in range(2):
            arrived(q_buf.at[1 - y_hi, SLOT[0], core], swap_recv.at[core])
        for dz in (2, 6, 1, 7):
            along_z(1, SLOT[0], dz, SLOT[NZ - dz])
        second_step(0)

        get_parents.wait()
        get_lengths.wait()
        get_lists.wait()
        slot_index = lax.broadcasted_iota(jnp.int32, (4, MAXP), 1)
        for b in range(BEAM):
            parent = parents[request * BEAM + b]
            lists[4 * b : 4 * b + 4, :] = jnp.broadcast_to(page_lists[pl.ds(parent, 1), :], (4, MAXP))
            room[4 * b : 4 * b + 4, :] = jnp.clip(lengths[parent] - slot_index * PAGE, 0, PAGE)
        chosen = lists[...]
        space = room[...]
        lane = lax.broadcasted_iota(jnp.int32, (4 * BEAM, KEYS), 1)
        for core in range(2):
            sign = 1 - 2 * core
            for kind, (dx, dy) in enumerate(key_moves):
                s_seq, s_head = place((x - sign * dx + 4) % 4, (y - sign * dy + 4) % 4, z, core)
                page = (s_seq * 32 + s_head) * 2
                live = [
                    jnp.sum(jnp.where(chosen == page + i, space, 0), axis=1, keepdims=True) for i in range(2)]
                seen = lane < jnp.where(lane < PAGE, live[0], live[1] + PAGE)
                cap[core, kind] = jnp.where(seen, jnp.inf, -jnp.inf)

        def attend(group, half, blocks):
            block = q_buf[(y_hi + group) % 2].reshape(ROWS, 2 * LAT + 128)
            rotary = block[:, 2 * LAT :]
            upper = jnp.where(lax.broadcasted_iota(jnp.int32, (ROWS, 128), 1) < ROPE, 0, 1)
            rows = jnp.concatenate([
                jnp.where(half == 0, block[:, :LAT], block[:, LAT : 2 * LAT]),
                jnp.where(upper == half, rotary, 0)], axis=1)
            many = len(blocks) * KEYS
            for i in range(0, len(blocks), 2):
                two = blocks[i : i + 2]
                columns = jnp.concatenate([keys[k] for k in two], axis=1)
                columns = jnp.concatenate([columns, columns[LAT:]], axis=0)
                raw = jnp.dot(rows, columns, preferred_element_type=F32)
                if two[0][2]:
                    limit = jnp.concatenate([cap[core, kind, pl.ds(16 * half, 16)] for core, kind, _ in two], axis=1)
                    raw = jnp.minimum(raw.reshape(2 * NZ, 16, 2 * KEYS), limit[None]).reshape(ROWS, 2 * KEYS)
                scores[:, i * KEYS : (i + 2) * KEYS] = raw
            peak = jnp.maximum(jnp.max(scores[:, :many], axis=1, keepdims=True), LOWEST)
            weights = jnp.exp2((scores[:, :many] - peak) * RATE)
            total = jnp.sum(weights, axis=1, keepdims=True)
            probs[:, :many] = weights.astype(BF16)
            values = jnp.concatenate([keys[core, kind, pooled, :LAT] for core, kind, pooled in blocks], axis=1)
            latent = lax.dot_general(
                probs[:, :many], values, (((1,), (1,)), ((), ())), preferred_element_type=F32)
            return peak, total, latent

        def store(group, half, result, in_lines):
            peak, total, latent = result
            side = (y_hi + group) % 2
            part[side, half] = latent.astype(BF16)
            if in_lines:
                zs_stat_src[...] = lines(peak, total)
            else:
                first = lax.broadcasted_iota(jnp.int32, (KEYS, KEYS), 1) == 0
                for i in range(2):
                    rows = slice(i * KEYS, (i + 1) * KEYS)
                    stat[side, half, i] = jnp.where(first, peak[rows], total[rows]).T[:8]

        def both(one, two):
            peak1, total1, latent1 = one
            peak2, total2, latent2 = two
            peak = jnp.maximum(peak1, peak2)
            keep1 = jnp.exp2((peak1 - peak) * RATE)
            keep2 = jnp.exp2((peak2 - peak) * RATE)
            return peak, total1 * keep1 + total2 * keep2, latent1 * keep1 + latent2 * keep2

        early = [(core, kind, 0) for core in range(2) for kind in range(4)] + [(0, 0, 1), (1, 0, 1)]
        late = [(core, kind, 1) for core in range(2) for kind in range(1, 4)]
        rs1_copies = {}

        def scatter(i, group, half):
            target = shifted(*scatter_moves[i])
            side = (y_hi + group) % 2
            rs1_copies[i, 2] = post(
                stat.at[side, half], rs1_stat.at[i], rs1_send.at[i, 2], rs1_recv.at[i, 2], target)
            for chunk in range(2):
                rows = pl.ds(KEYS * chunk, KEYS)
                rs1_copies[i, chunk] = post(
                    part.at[side, half, rows], rs1.at[i, rows], rs1_send.at[i, chunk], rs1_recv.at[i, chunk], target)

        second_step(1)
        for slot in (SLOT[0], SLOT[1], SLOT[7], SLOT[3], SLOT[5], SLOT[4]):
            await_slot(0, slot)
        own_prompt.wait()
        for piece in range(3):
            await_keys(piece, True)
        await_keys(0, False)
        early_z = attend(0, 1 - x_hi, early)
        early_y = attend(0, x_hi, early)
        for slot in (SLOT[1], SLOT[7], SLOT[3], SLOT[5], SLOT[4]):
            await_slot(1, slot)
        early_x = attend(1, 1 - x_hi, early)
        await_keys(1, False)
        await_keys(2, False)
        store(0, 1 - x_hi, both(early_z, attend(0, 1 - x_hi, late)), True)
        zs_copies = []
        for slot in range(NZ - 1):
            target = up(RELATIVE[slot])
            zs_copies.append(post(
                part.at[y_hi, 1 - x_hi, pl.ds(BLOCK * slot, BLOCK)], zs.at[slot],
                zs_send.at[slot, 0], zs_recv.at[slot, 0], target))
            zs_copies.append(post(
                zs_stat_src.at[slot], zs_stat.at[slot], zs_send.at[slot, 1], zs_recv.at[slot, 1], target))
        store(0, x_hi, both(early_y, attend(0, x_hi, late)), False)
        scatter(0, 0, x_hi)
        store(1, 1 - x_hi, both(early_x, attend(1, 1 - x_hi, late)), False)
        scatter(1, 1, 1 - x_hi)
        store(1, x_hi, attend(1, x_hi, early + late), False)

        rs2_copies = []

        def home(slot, target):
            rs2_copies.append(post(
                rs2_src.at[slot], rs2.at[slot], rs2_send.at[slot, 0], rs2_recv.at[slot, 0], target))
            rs2_copies.append(post(
                rs2_stat_src.at[slot], rs2_stat.at[slot], rs2_send.at[slot, 1], rs2_recv.at[slot, 1], target))

        for i in range(2):
            rs1_copies[i, 2].wait_recv()
        for chunk in range(2):
            rows = slice(chunk * KEYS, (chunk + 1) * KEYS)
            for i in range(2):
                rs1_copies[i, chunk].wait_recv()
            columns = jnp.concatenate([
                stat[1 - y_hi, x_hi, chunk], rs1_stat[0, chunk], rs1_stat[1, chunk], jnp.zeros((KEYS - 24, KEYS), F32),
            ], axis=0).T
            peak, total, latent = merge(
                [part[1 - y_hi, x_hi, rows], rs1[0, rows], rs1[1, rows]],
                [(columns[:, 8 * i : 8 * i + 1], columns[:, 8 * i + 1 : 8 * i + 2]) for i in range(3)])
            rs2_src[4 * chunk : 4 * chunk + 4] = latent.astype(BF16).reshape(4, BLOCK, LAT)
            rs2_stat_src[4 * chunk : 4 * chunk + 4] = lines(peak, total)
            for slot in range(4 * chunk, 4 * chunk + 4):
                home(slot, place(x, 3 - y, (z + RELATIVE[slot]) % NZ, 1))
        for copy in zs_copies:
            copy.wait_recv()
        peak, total, latent = merge(
            [part[y_hi, 1 - x_hi, BLOCK * SLOT[0] :]] + [zs[slot] for slot in range(NZ - 1)],
            [from_line(zs_stat_src[SLOT[0]])] + [from_line(zs_stat[slot]) for slot in range(NZ - 1)])
        rs2_src[NZ] = latent.astype(BF16)
        rs2_stat_src[NZ : NZ + 1] = lines(peak, total)
        home(NZ, out_place(2, 1, 1))
        own_v.wait()
        arrived(v_buf.at[0], v_recv)
        for copy in rs2_copies:
            copy.wait_recv()
        peak, total, latent = merge(
            [rs2[slot] for slot in range(NZ + 1)], [from_line(rs2_stat[slot]) for slot in range(NZ + 1)])
        latent = (latent / total).astype(BF16)
        row = lax.broadcasted_iota(jnp.int32, (16, VDIM), 0)
        place_out = mirror_request * 2 + x_hi
        out_copies = []
        for core in range(2):
            attended = jnp.zeros((16, VDIM), F32)
            for h in range(4):
                product = jnp.dot(latent[16 * core : 16 * core + 16], v_buf[core, h], preferred_element_type=F32)
                attended = jnp.where(row % 4 == h, product, attended)
            out_src[core] = attended.astype(BF16)
            for i, (dx, dy) in enumerate(out_moves):
                if core == 0 or i > 0:
                    copy = post(
                        out_src.at[core], out.at[place_out], out_send.at[core, i], out_recv.at[i],
                        out_place(dx, dy, core))
                    if core == 1:
                        out_copies.append(copy)
        out[place_out] = out_src[1]
        for copy in out_copies:
            copy.wait_recv()
        for copy in work:
            copy.wait_send()

    for copy in copies:
        copy.wait_send()


def body(queries, prompt_latent, pool_latent, value_up, parents, page_lists, lengths):
    vmem = pl.BlockSpec(memory_space=pltpu.VMEM)
    hbm = pl.BlockSpec(memory_space=pltpu.HBM)
    operands = (parents, lengths, page_lists, queries, prompt_latent.swapaxes(1, 2), pool_latent, value_up)
    dma = pltpu.SemaphoreType.DMA
    result = pl.pallas_call(
        kernel,
        out_shape=pltpu.VMEM((8, 16, VDIM), BF16),
        in_specs=[hbm] * 7,
        out_specs=vmem,
        scratch_shapes=[
            pltpu.SMEM((32,), jnp.int32),
            pltpu.SMEM((32,), jnp.int32),
            pltpu.VMEM((32, MAXP), jnp.int32),
            pltpu.VMEM((2, BEAM, 4, WIDTH), BF16),
            pltpu.VMEM((2, 16, 2 * LAT + 128), F32),
            pltpu.VMEM((16, 2 * LAT + 128), BF16),
            pltpu.VMEM((16, 2 * LAT + 128), BF16),
            pltpu.VMEM((2, NZ, 2, 16, 2 * LAT + 128), BF16),
            pltpu.VMEM((2, PAGE, WIDTH), BF16),
            pltpu.VMEM((WIDTH, KEYS), BF16),
            pltpu.VMEM((2, 4, 2, WIDTH, KEYS), BF16),
            pltpu.VMEM((2, 4, LAT, VDIM), BF16),
            pltpu.VMEM((4 * BEAM, MAXP), jnp.int32),
            pltpu.VMEM((4 * BEAM, MAXP), jnp.int32),
            pltpu.VMEM((2, 4, 4 * BEAM, KEYS), F32),
            pltpu.VMEM((ROWS, 16 * KEYS), F32),
            pltpu.VMEM((ROWS, 16 * KEYS), BF16),
            pltpu.VMEM((2, 2, ROWS, LAT), BF16),
            pltpu.VMEM((2, 2, 2, 8, KEYS), F32),
            pltpu.VMEM((2, ROWS, LAT), BF16),
            pltpu.VMEM((2, 2, 8, KEYS), F32),
            pltpu.VMEM((NZ - 1, BLOCK, LAT), BF16),
            pltpu.VMEM((NZ, 1, KEYS), F32),
            pltpu.VMEM((NZ - 1, 1, KEYS), F32),
            pltpu.VMEM((NZ + 1, BLOCK, LAT), BF16),
            pltpu.VMEM((NZ + 1, 1, KEYS), F32),
            pltpu.VMEM((NZ + 1, BLOCK, LAT), BF16),
            pltpu.VMEM((NZ + 1, 1, KEYS), F32),
            pltpu.VMEM((2, 16, VDIM), BF16),
            dma((8,)), dma((4, 3)), dma((2, 4, 3)), dma, dma((2,)), dma((5,)), dma((2, NZ)), dma((2, NZ)), dma((2, NZ)),
            dma, dma, dma((2, 3)), dma((2, 3)), dma((NZ - 1, 2)), dma((NZ - 1, 2)), dma((NZ + 1, 2)), dma((NZ + 1, 2)),
            dma((2, 8)), dma((8,)),
        ],
        compiler_params=pltpu.CompilerParams(
            collective_id=0, has_side_effects=True, vmem_limit_bytes=48 * 2**20
        ),
    )(
        *[pltpu.with_memory_space_constraint(operand, pltpu.HBM) for operand in operands]
    )
    return result.reshape(32, 4, VDIM)


def solution(mesh):
    return jax.shard_map(
        body,
        mesh=mesh,
        in_specs=(
            P(None, "head", None),
            P(None, ("seq", "head"), None),
            P(("seq", "head"), None, None),
            P("head", None, None),
            P(),
            P(),
            P(),
        ),
        out_specs=P(None, "head", None),
        check_vma=False,
    )
```

time: 395 us -> 43.9 us (0.11)
  the two profiles are of different devices: /device:TPU:8 before, /device:TPU:1 now
where the time goes in v6:
time: 43.9 us; the launch traced here: 43.8 us
  Pallas kernels  43.2 us (98%)
  local copies, waits for them, and re-layouts  0.62 us (1%)
    pallas_call x1, Pallas kernels, body(): pl.pallas_call(kernel, out_shape=pltpu.VMEM((8, 16, VDIM), BF16), in_spec...  43.2 us

profile of v6, /device:TPU:1, one launch (start us, length us, event | category | flops | bytes accessed | tf_op | source)
XLA Modules:
  0.0 43.8 jit_solution(560318216418992744)
XLA Ops:
  0.0 43.2 %shard_map.73 = bf16[8,16,128]{2,1,0:T(8,128)(2,1)S(1)} custom-call(s32[32]{0:T(128)} %parents_hbm.1, s32[32]{0:T(128)} %lengths_hbm.1, s32[32,64]{1,0:T(8,128)} %lists_hbm.1, bf16[32,4,576]{2,1,0:T(4,128)(2,1)} %queries.1, bf16[4,576,128]{2,1,0:T(8,128)(2,1)} %bitcast.3, bf16[2,64,576]{2,1,0:T(8,128)(2,1)} %pool.1, bf16[4,512,128]{2,1,0:T(8,128)(2,1)} %value_up.1), custom_call_target="tpu_custom_call" | custom-call | tf_op jit(solution)/shard_map/pallas_call | solution.py:437
  43.2 0.6 %copy.9 = bf16[32,4,128]{2,1,0:T(4,128)(2,1)} copy(bf16[32,4,128]{2,1,0:T(4,128)(2,1)S(1)} %bitcast.2) | data formatting | bytes 65536

commit v7 on v5

--- a/solution.py
+++ b/solution.py
@@ -43,16 +43,16 @@
     return peak, total, latent
 
 
-def lines(peak, total):
+def lines(peak, total, start=0):
     rows = peak.shape[0]
-    lane = lax.broadcasted_iota(jnp.int32, (rows, KEYS), 1)
+    lane = lax.broadcasted_iota(jnp.int32, (rows, KEYS), 1) - start
     row = lax.broadcasted_iota(jnp.int32, (rows, KEYS), 0) % 16
     spread = jnp.where(lane == row, peak, 0.0) + jnp.where(lane == row + 16, total, 0.0)
     return jnp.sum(spread.reshape(rows // 16, 16, KEYS), axis=1, keepdims=True)
 
 
-def from_line(line):
-    lane = lax.broadcasted_iota(jnp.int32, (16, KEYS), 1)
+def from_line(line, start=0):
+    lane = lax.broadcasted_iota(jnp.int32, (16, KEYS), 1) - start
     row = lax.broadcasted_iota(jnp.int32, (16, KEYS), 0)
     return (
         jnp.sum(jnp.where(lane == row, line, 0.0), axis=1, keepdims=True),
@@ -66,7 +66,7 @@
     q_in, q_wide, q_mirror, q_buf, pool_in, keys, v_buf, lists, room, cap, scores, probs,
     part, stat, rs1, rs1_stat, zs, zs_stat_src, zs_stat, rs2_src, rs2_stat_src, rs2, rs2_stat, out_src,
     local_sem, key_send, key_recv, core_send, core_recv, swap_send, swap_recv, q_send, q_recv,
-    rs1_send, rs1_recv, zs_send, zs_recv, rs2_send, rs2_recv, out_send, out_recv,
+    v_send, v_recv, rs1_send, rs1_recv, zs_send, zs_recv, rs2_send, rs2_recv, out_send, out_recv,
 ):
     seq = lax.axis_index("seq")
     head = lax.axis_index("head")
@@ -81,17 +81,17 @@
     step = 1 - 2 * c
     request = x_lo * 2 + y_lo
 
-    def shifted(dx, dy, sign=1):
-        return place((x + sign * dx + 4) % 4, (y + sign * dy + 4) % 4, z, c)
+    def shifted(dx, dy, sign=1, core=c):
+        return place((x + sign * dx + 4) % 4, (y + sign * dy + 4) % 4, z, core)
 
     other_core = place(x, y, z, 1 - c)
     mirror = place(x, 3 - y, z, c)
     key_moves = ((1, 0), (0, 1), (1, 1))
     scatter_moves = ((0, 2), (2, 0))
-    out_moves = [(dx, dy) for dy in range(2) for dx in range(4) if (dx, dy) != (0, 0)]
-
-    def out_place(dx, dy):
-        return place((x + dx) % 4, y_hi * 2 + (y_lo + dy) % 2, z, c)
+    out_moves = [(dx, dy) for dy in range(2) for dx in range(4)]
+
+    def out_place(dx, dy, core):
+        return place((x + dx) % 4, y_hi * 2 + (y_lo + dy) % 2, z, core)
 
     barrier = pltpu.get_barrier_semaphore()
     senders = [place(x, y, (z + dz) % NZ, c) for dz in (2, 6, 1, 7)]
@@ -106,7 +106,7 @@
     mirror_q = pltpu.make_async_copy(queries.at[pl.ds(mirror_request * BEAM, BEAM)], q_in.at[1], local_sem.at[1])
     own_pool = pltpu.make_async_copy(pool, pool_in, local_sem.at[2])
     own_prompt = pltpu.make_async_copy(prompt.at[request], keys.at[c, 0, 0], local_sem.at[3])
-    own_v = pltpu.make_async_copy(value_up, v_buf, local_sem.at[4])
+    own_v = pltpu.make_async_copy(value_up, v_buf.at[1], local_sem.at[4])
     get_parents = pltpu.make_async_copy(parents_hbm, parents, local_sem.at[5])
     get_lengths = pltpu.make_async_copy(lengths_hbm, lengths, local_sem.at[6])
     get_lists = pltpu.make_async_copy(lists_hbm, page_lists, local_sem.at[7])
@@ -142,13 +142,18 @@
 
     copies = []
 
-    def send(src, dst, send_sem, recv_sem, target):
-        copy = pltpu.make_async_remote_copy(
-            src_ref=src, dst_ref=dst, send_sem=send_sem, recv_sem=recv_sem, device_id=target, device_id_type=MESH
-        )
+    def describe(src, dst, send_sem, recv_sem, target):
+        return pltpu.make_async_remote_copy(
+            src_ref=src, dst_ref=dst, send_sem=send_sem, recv_sem=recv_sem, device_id=target, device_id_type=MESH)
+
+    def send(*what):
+        copy = describe(*what)
         copy.start()
         copies.append(copy)
         return copy
+
+    def arrived(dst, recv_sem):
+        describe(dst, dst, v_send, recv_sem, other_core).wait_recv()
 
     swap = send(q_mirror, q_buf.at[y_hi, SLOT[0]], swap_send, swap_recv, mirror)
     q_copies = {}
@@ -285,16 +290,14 @@
                 zs_stat_src[half] = lines(peak[half_rows], total[half_rows])
 
     def scatter(i, group, half):
-        target = shifted(*scatter_moves[i])
-        rs1_copies[i, CHUNKS] = send(
-            stat.at[group, half], rs1_stat.at[i], rs1_send.at[i, CHUNKS], rs1_recv.at[i, CHUNKS], target)
+        target = shifted(*scatter_moves[i], core=1)
+        send(stat.at[group, half], rs1_stat.at[i, c], rs1_send.at[i, CHUNKS], rs1_recv.at[i, c, CHUNKS], target)
         for chunk in range(CHUNKS):
             rows = pl.ds(CHUNK * chunk, CHUNK)
-            rs1_copies[i, chunk] = send(
-                part.at[group, half, rows], rs1.at[i, rows], rs1_send.at[i, chunk], rs1_recv.at[i, chunk], target)
-
-    rs1_copies = {}
-    zs_copies = []
+            send(
+                part.at[group, half, rows], rs1.at[i, c, rows],
+                rs1_send.at[i, chunk], rs1_recv.at[i, c, chunk], target)
+
     wait_queries(0)
     wait_core(0)
     prompt_a = attend(y_hi, 0)
@@ -307,66 +310,125 @@
     wait_core(2)
     finish(y_hi, prompt_a, True)
     for slot in range(NZ - 1):
-        target = place(x, y, (z + RELATIVE[slot]) % NZ, c)
-        zs_copies.append(send(
-            part.at[y_hi, 1 - x_hi, pl.ds(16 * slot, 16)], zs.at[slot], zs_send.at[slot, 0], zs_recv.at[slot, 0], target))
-        zs_copies.append(send(
-            zs_stat_src.at[1 - x_hi, slot], zs_stat.at[slot], zs_send.at[slot, 1], zs_recv.at[slot, 1], target))
+        target = place(x, y, (z + RELATIVE[slot]) % NZ, 1)
+        send(
+            part.at[y_hi, 1 - x_hi, pl.ds(16 * slot, 16)], zs.at[slot, c],
+            zs_send.at[slot, 0], zs_recv.at[c, slot, 0], target)
+        send(
+            zs_stat_src.at[1 - x_hi, slot], zs_stat.at[slot, c], zs_send.at[slot, 1], zs_recv.at[c, slot, 1], target)
     scatter(0, y_hi, x_hi)
     finish(1 - y_hi, prompt_b, False)
     scatter(1, 1 - y_hi, 1 - x_hi)
-
-    rs2_copies = []
-
-    def home(slot, target):
-        rs2_copies.append(send(
-            rs2_src.at[slot], rs2.at[slot], rs2_send.at[slot, 0], rs2_recv.at[slot, 0], target))
-        rs2_copies.append(send(
-            rs2_stat_src.at[slot], rs2_stat.at[slot], rs2_send.at[slot, 1], rs2_recv.at[slot, 1], target))
-
-    for i in range(2):
-        rs1_copies[i, CHUNKS].wait_recv()
-    columns = jnp.concatenate([
-        stat[1 - y_hi, x_hi], rs1_stat[0], rs1_stat[1], jnp.zeros((KEYS - 24, KEYS), F32)], axis=0).T
-    per = CHUNK // 16
-    for chunk in range(CHUNKS):
-        rows = slice(chunk * CHUNK, (chunk + 1) * CHUNK)
-        for i in range(2):
-            rs1_copies[i, chunk].wait_recv()
-        peak, total, latent = merge(
-            [part[1 - y_hi, x_hi, rows], rs1[0, rows], rs1[1, rows]],
-            [(columns[rows, 8 * i : 8 * i + 1], columns[rows, 8 * i + 1 : 8 * i + 2]) for i in range(3)])
-        rs2_src[per * chunk : per * chunk + per] = latent.astype(BF16).reshape(per, 16, LAT)
-        rs2_stat_src[per * chunk : per * chunk + per] = lines(peak, total)
-        for slot in range(per * chunk, per * chunk + per):
-            home(slot, place(x, 3 - y, (z + RELATIVE[slot]) % NZ, c))
-    for copy in zs_copies:
-        copy.wait_recv()
-    peak, total, latent = merge(
-        [part[y_hi, 1 - x_hi, 16 * SLOT[0] :]] + [zs[slot] for slot in range(NZ - 1)],
-        [from_line(zs_stat_src[1 - x_hi, SLOT[0]])] + [from_line(zs_stat[slot]) for slot in range(NZ - 1)])
-    rs2_src[NZ] = latent.astype(BF16)
-    rs2_stat_src[NZ : NZ + 1] = lines(peak, total)
-    home(NZ, place((x + 2) % 4, y_hi * 2 + 1 - y_lo, z, c))
     own_v.wait()
-    for copy in rs2_copies:
-        copy.wait_recv()
-    peak, total, latent = merge([rs2[slot] for slot in range(NZ + 1)], [from_line(rs2_stat[slot]) for slot in range(NZ + 1)])
-    latent = (latent / total).astype(BF16)
-    attended = jnp.zeros((16, VDIM), F32)
-    row = lax.broadcasted_iota(jnp.int32, (16, VDIM), 0)
-    for h in range(4):
-        product = jnp.dot(latent, v_buf[h], preferred_element_type=F32)
-        attended = jnp.where(row % 4 == h, product, attended)
-    out_src[...] = attended.astype(BF16)
-    place_out = mirror_request * 2 + x_hi
-    out_copies = []
-    for i, (dx, dy) in enumerate(out_moves):
-        out_copies.append(send(
-            out_src, out.at[place_out], out_send.at[i], out_recv.at[i], out_place(dx, dy)))
-    out[place_out] = out_src[...]
-    for copy in out_copies:
-        copy.wait_recv()
+    last = SLOT[0]
+
+    @pl.when(c == 0)
+    def _():
+        mine = [
+            describe(
+                part.at[y_hi, 1 - x_hi, pl.ds(16 * last, 16)], zs.at[last, 0],
+                zs_send.at[last, 0], zs_recv.at[0, last, 0], other_core),
+            describe(
+                zs_stat_src.at[1 - x_hi, last], zs_stat.at[last, 0],
+                zs_send.at[last, 1], zs_recv.at[0, last, 1], other_core),
+            describe(part.at[1 - y_hi, x_hi], rs1.at[2, 0], rs1_send.at[2, 0], rs1_recv.at[2, 0, 0], other_core),
+            describe(stat.at[1 - y_hi, x_hi], rs1_stat.at[2, 0], rs1_send.at[2, 1], rs1_recv.at[2, 0, 1], other_core),
+            describe(value_up, v_buf.at[0], v_send, v_recv, other_core),
+        ]
+        for copy in mine:
+            copy.start()
+        for i in range(8):
+            arrived(out.at[0], out_recv.at[i])
+        for copy in mine:
+            copy.wait_send()
+
+    @pl.when(c == 1)
+    def _():
+        work = []
+
+        def post(*what):
+            copy = describe(*what)
+            copy.start()
+            work.append(copy)
+            return copy
+
+        zs[last, 1] = part[y_hi, 1 - x_hi, 16 * last :]
+        zs_stat[last, 1] = zs_stat_src[1 - x_hi, last]
+        rs2_copies = []
+
+        def home(slot, target):
+            rs2_copies.append(post(
+                rs2_src.at[slot], rs2.at[slot], rs2_send.at[slot, 0], rs2_recv.at[slot, 0], target))
+            rs2_copies.append(post(
+                rs2_stat_src.at[slot], rs2_stat.at[slot], rs2_send.at[slot, 1], rs2_recv.at[slot, 1], target))
+
+        per = CHUNK // 16
+        for chunk in range(CHUNKS):
+            rows = slice(chunk * CHUNK, (chunk + 1) * CHUNK)
+            here = slice(chunk * per, (chunk + 1) * per)
+            both = []
+            for core in range(2):
+                if chunk == 0:
+                    for i in range(2):
+                        arrived(rs1_stat.at[i, core], rs1_recv.at[i, core, CHUNKS])
+                    if core == 0:
+                        arrived(rs1.at[2, 0], rs1_recv.at[2, 0, 0])
+                        arrived(rs1_stat.at[2, 0], rs1_recv.at[2, 0, 1])
+                for i in range(2):
+                    arrived(rs1.at[i, core, pl.ds(CHUNK * chunk, CHUNK)], rs1_recv.at[i, core, chunk])
+                kept = part[1 - y_hi, x_hi, rows] if core else rs1[2, 0, rows]
+                kept_stat = stat[1 - y_hi, x_hi] if core else rs1_stat[2, 0]
+                columns = jnp.concatenate([
+                    kept_stat, rs1_stat[0, core], rs1_stat[1, core], jnp.zeros((KEYS - 24, KEYS), F32)], axis=0).T[rows]
+                peak, total, latent = merge(
+                    [kept, rs1[0, core, rows], rs1[1, core, rows]],
+                    [(columns[:, 8 * i : 8 * i + 1], columns[:, 8 * i + 1 : 8 * i + 2]) for i in range(3)])
+                rs2_src[here, core] = latent.astype(BF16).reshape(per, 16, LAT)
+                both.append(lines(peak, total, 32 * core))
+            rs2_stat_src[here] = both[0] + both[1]
+            for slot in range(per * chunk, per * chunk + per):
+                home(slot, place(x, 3 - y, (z + RELATIVE[slot]) % NZ, 1))
+        both = []
+        for core in range(2):
+            for slot in range(NZ):
+                if core == 0 or slot != last:
+                    arrived(zs.at[slot, core], zs_recv.at[core, slot, 0])
+                    arrived(zs_stat.at[slot, core], zs_recv.at[core, slot, 1])
+            peak, total, latent = merge(
+                [zs[slot, core] for slot in range(NZ)], [from_line(zs_stat[slot, core]) for slot in range(NZ)])
+            rs2_src[NZ, core] = latent.astype(BF16)
+            both.append(lines(peak, total, 32 * core))
+        rs2_stat_src[NZ : NZ + 1] = both[0] + both[1]
+        home(NZ, out_place(2, 1, 1))
+        arrived(v_buf.at[0], v_recv)
+        for copy in rs2_copies:
+            copy.wait_recv()
+        row = lax.broadcasted_iota(jnp.int32, (16, VDIM), 0)
+        place_out = mirror_request * 2 + x_hi
+        out_copies = []
+        for core in range(2):
+            peak, total, latent = merge(
+                [rs2[slot, core] for slot in range(NZ + 1)],
+                [from_line(rs2_stat[slot], 32 * core) for slot in range(NZ + 1)])
+            latent = (latent / total).astype(BF16)
+            attended = jnp.zeros((16, VDIM), F32)
+            for h in range(4):
+                product = jnp.dot(latent, v_buf[core, h], preferred_element_type=F32)
+                attended = jnp.where(row % 4 == h, product, attended)
+            out_src[core] = attended.astype(BF16)
+            for i, (dx, dy) in enumerate(out_moves):
+                if core == 0 or i > 0:
+                    copy = post(
+                        out_src.at[core], out.at[place_out], out_send.at[core, i], out_recv.at[i],
+                        out_place(dx, dy, core))
+                    if core == 1:
+                        out_copies.append(copy)
+        out[place_out] = out_src[1]
+        for copy in out_copies:
+            copy.wait_recv()
+        for copy in work:
+            copy.wait_send()
+
     for copy in copies:
         copy.wait_send()
 
@@ -391,7 +453,7 @@
             pltpu.VMEM((2, NZ, 16, 2 * LAT + 128), BF16),
             pltpu.VMEM((2, PAGE, WIDTH), BF16),
             pltpu.VMEM((2, 4, 2, WIDTH, KEYS), BF16),
-            pltpu.VMEM((4, LAT, VDIM), BF16),
+            pltpu.VMEM((2, 4, LAT, VDIM), BF16),
             pltpu.VMEM((4 * BEAM, MAXP), jnp.int32),
             pltpu.VMEM((4 * BEAM, MAXP), jnp.int32),
             pltpu.VMEM((4 * BEAM, 8 * KEYS), F32),
@@ -399,18 +461,20 @@
             pltpu.VMEM((2 * KEYS, 8 * KEYS), BF16),
             pltpu.VMEM((2, 2, KEYS, LAT), BF16),
             pltpu.VMEM((2, 2, 8, KEYS), F32),
-            pltpu.VMEM((2, KEYS, LAT), BF16),
-            pltpu.VMEM((2, 8, KEYS), F32),
-            pltpu.VMEM((NZ - 1, 16, LAT), BF16),
+            pltpu.VMEM((3, 2, KEYS, LAT), BF16),
+            pltpu.VMEM((3, 2, 8, KEYS), F32),
+            pltpu.VMEM((NZ, 2, 16, LAT), BF16),
             pltpu.VMEM((2, NZ, 1, KEYS), F32),
-            pltpu.VMEM((NZ - 1, 1, KEYS), F32),
-            pltpu.VMEM((NZ + 1, 16, LAT), BF16),
+            pltpu.VMEM((NZ, 2, 1, KEYS), F32),
+            pltpu.VMEM((NZ + 1, 2, 16, LAT), BF16),
             pltpu.VMEM((NZ + 1, 1, KEYS), F32),
-            pltpu.VMEM((NZ + 1, 16, LAT), BF16),
+            pltpu.VMEM((NZ + 1, 2, 16, LAT), BF16),
             pltpu.VMEM((NZ + 1, 1, KEYS), F32),
-            pltpu.VMEM((16, VDIM), BF16),
+            pltpu.VMEM((2, 16, VDIM), BF16),
             dma((8,)), dma((3, 3)), dma((3, 3)), dma((4, 3)), dma((4, 3)), dma, dma, dma((2, NZ)), dma((2, NZ)),
-            dma((2, CHUNKS + 1)), dma((2, CHUNKS + 1)), dma((NZ - 1, 2)), dma((NZ - 1, 2)), dma((NZ + 1, 2)), dma((NZ + 1, 2)), dma((7,)), dma((7,)),
+            dma, dma,
+            dma((3, CHUNKS + 1)), dma((3, 2, CHUNKS + 1)), dma((NZ, 2)), dma((2, NZ, 2)), dma((NZ + 1, 2)), dma((NZ + 1, 2)),
+            dma((2, 8)), dma((8,)),
         ],
         compiler_params=pltpu.CompilerParams(
             collective_id=0, has_side_effects=True, vmem_limit_bytes=48 * 2**20

time: 41.5 us -> 42.6 us (1.027)
  the two profiles are of different devices: /device:TPU:8 before, /device:TPU:1 now
where the time goes in v7:
time: 42.6 us
  Pallas kernels  41.9 us (98%)
  local copies, waits for them, and re-layouts  0.62 us (1%)
    pallas_call x1, Pallas kernels, body(): pl.pallas_call(kernel, out_shape=pltpu.VMEM((8, 16, VDIM), BF16), in_spec...  41.9 us

profile of v7, /device:TPU:1, one launch (start us, length us, event | category | flops | bytes accessed | tf_op | source)
XLA Modules:
  0.0 42.6 jit_solution(18128140388699874442)
XLA Ops:
  0.0 41.9 %shard_map.73 = bf16[8,16,128]{2,1,0:T(8,128)(2,1)S(1)} custom-call(s32[32]{0:T(128)} %parents_hbm.1, s32[32]{0:T(128)} %lengths_hbm.1, s32[32,64]{1,0:T(8,128)} %lists_hbm.1, bf16[32,4,576]{2,1,0:T(4,128)(2,1)} %queries.1, bf16[4,576,128]{2,1,0:T(8,128)(2,1)} %bitcast.3, bf16[2,64,576]{2,1,0:T(8,128)(2,1)} %pool.1, bf16[4,512,128]{2,1,0:T(8,128)(2,1)} %value_up.1), custom_call_target="tpu_custom_call" | custom-call | tf_op jit(solution)/shard_map/pallas_call | solution.py:441
  41.9 0.6 %copy.9 = bf16[32,4,128]{2,1,0:T(4,128)(2,1)} copy(bf16[32,4,128]{2,1,0:T(4,128)(2,1)S(1)} %bitcast.2) | data formatting | bytes 65536

commit v8 on v5

--- a/solution.py
+++ b/solution.py
@@ -306,13 +306,13 @@
     wait_core(1)
     wait_core(2)
     finish(y_hi, prompt_a, True)
+    scatter(0, y_hi, x_hi)
     for slot in range(NZ - 1):
         target = place(x, y, (z + RELATIVE[slot]) % NZ, c)
         zs_copies.append(send(
             part.at[y_hi, 1 - x_hi, pl.ds(16 * slot, 16)], zs.at[slot], zs_send.at[slot, 0], zs_recv.at[slot, 0], target))
         zs_copies.append(send(
             zs_stat_src.at[1 - x_hi, slot], zs_stat.at[slot], zs_send.at[slot, 1], zs_recv.at[slot, 1], target))
-    scatter(0, y_hi, x_hi)
     finish(1 - y_hi, prompt_b, False)
     scatter(1, 1 - y_hi, 1 - x_hi)
 

time: 41.5 us -> 41.6 us (level)
  no operation moved by 1% of the time
where the time goes in v8:
time: 41.6 us; the launch traced here: 41.5 us
  Pallas kernels  40.8 us (98%)
  local copies, waits for them, and re-layouts  0.62 us (1%)
    pallas_call x1, Pallas kernels, body(): pl.pallas_call(kernel, out_shape=pltpu.VMEM((8, 16, VDIM), BF16), in_spec...  40.8 us

profile of v8, /device:TPU:8, one launch (start us, length us, event | category | flops | bytes accessed | tf_op | source)
XLA Modules:
  0.0 41.5 jit_solution(16861673403511594705)
XLA Ops:
  0.0 40.8 %shard_map.73 = bf16[8,16,128]{2,1,0:T(8,128)(2,1)S(1)} custom-call(s32[32]{0:T(128)} %parents_hbm.1, s32[32]{0:T(128)} %lengths_hbm.1, s32[32,64]{1,0:T(8,128)} %lists_hbm.1, bf16[32,4,576]{2,1,0:T(4,128)(2,1)} %queries.1, bf16[4,576,128]{2,1,0:T(8,128)(2,1)} %bitcast.3, bf16[2,64,576]{2,1,0:T(8,128)(2,1)} %pool.1, bf16[4,512,128]{2,1,0:T(8,128)(2,1)} %value_up.1), custom_call_target="tpu_custom_call" | custom-call | tf_op jit(solution)/shard_map/pallas_call | solution.py:379
  40.8 0.6 %copy.9 = bf16[32,4,128]{2,1,0:T(4,128)(2,1)} copy(bf16[32,4,128]{2,1,0:T(4,128)(2,1)S(1)} %bitcast.2) | data formatting | bytes 65536

commit v9 on v8

--- a/solution.py
+++ b/solution.py
@@ -97,6 +97,7 @@
     senders = [place(x, y, (z + dz) % NZ, c) for dz in (2, 6, 1, 7)]
     senders += [shifted(dx * step, dy * step, -1) for dx, dy in key_moves]
     senders += [shifted(dx, dy) for dx, dy in scatter_moves]
+    senders += [place(x, 3 - y, (z + dz) % NZ, c) for dz in (2, 6)]
     senders += [mirror, other_core]
     for sender in senders:
         pl.semaphore_signal(barrier, inc=1, device_id=sender, device_id_type=MESH)
@@ -159,8 +160,8 @@
             q_buf.at[side, source], q_buf.at[side, slot],
             q_send.at[group, slot], q_recv.at[group, slot], place(x, y, (z + dz + NZ) % NZ, c))
 
-    def first_step(group):
-        for dz in (2, 6, 1, 7):
+    def first_step(group, steps):
+        for dz in steps:
             along_z(group, SLOT[0], dz, SLOT[NZ - dz])
 
     def second_step(group):
@@ -174,7 +175,12 @@
         for dz in (1, 7, 3, 5, 4):
             q_copies[group, SLOT[dz]].wait_recv()
 
-    first_step(0)
+    first_step(0, (2, 6))
+    for dz in (2, 6):
+        slot = SLOT[NZ - dz]
+        q_copies[1, slot] = send(
+            q_mirror, q_buf.at[y_hi, slot], q_send.at[1, slot], q_recv.at[1, slot], place(x, 3 - y, (z + dz) % NZ, c))
+    first_step(0, (1, 7))
     pieces = ((0, slice(0, WIDTH)), (1, slice(0, WIDTH // 2)), (1, slice(WIDTH // 2, WIDTH)))
     key_copies = {}
 
@@ -230,13 +236,13 @@
             seen = lane < jnp.where(lane < PAGE, live[0], live[1] + PAGE)
             cap[:, (cc * 4 + kind) * KEYS : (cc * 4 + kind + 1) * KEYS] = jnp.where(seen, jnp.inf, -jnp.inf)
 
+    second_step(0)
+    second_step(1)
     swap.wait_recv()
-    first_step(1)
-    second_step(0)
+    first_step(1, (1, 7))
     for kind in range(1, 4):
         key_copies[kind, 0].wait_recv()
         to_core(kind, 0)
-    second_step(1)
     for kind in range(1, 4):
         key_copies[kind, 1].wait_recv()
         to_core(kind, 1)

time: 41.6 us -> 41.5 us (level)
  no operation moved by 1% of the time
where the time goes in v9:
time: 41.5 us; the launch traced here: 41.4 us
  Pallas kernels  40.8 us (98%)
  local copies, waits for them, and re-layouts  0.62 us (1%)
    pallas_call x1, Pallas kernels, body(): pl.pallas_call(kernel, out_shape=pltpu.VMEM((8, 16, VDIM), BF16), in_spec...  40.8 us

profile of v9, /device:TPU:8, one launch (start us, length us, event | category | flops | bytes accessed | tf_op | source)
XLA Modules:
  0.0 41.4 jit_solution(18016112845358392728)
XLA Ops:
  0.0 40.8 %shard_map.73 = bf16[8,16,128]{2,1,0:T(8,128)(2,1)S(1)} custom-call(s32[32]{0:T(128)} %parents_hbm.1, s32[32]{0:T(128)} %lengths_hbm.1, s32[32,64]{1,0:T(8,128)} %lists_hbm.1, bf16[32,4,576]{2,1,0:T(4,128)(2,1)} %queries.1, bf16[4,576,128]{2,1,0:T(8,128)(2,1)} %bitcast.3, bf16[2,64,576]{2,1,0:T(8,128)(2,1)} %pool.1, bf16[4,512,128]{2,1,0:T(8,128)(2,1)} %value_up.1), custom_call_target="tpu_custom_call" | custom-call | tf_op jit(solution)/shard_map/pallas_call | solution.py:385
  40.8 0.6 %copy.9 = bf16[32,4,128]{2,1,0:T(4,128)(2,1)} copy(bf16[32,4,128]{2,1,0:T(4,128)(2,1)S(1)} %bitcast.2) | data formatting | bytes 65536

commit v10 on v9

--- a/solution.py
+++ b/solution.py
@@ -238,11 +238,11 @@
 
     second_step(0)
     second_step(1)
-    swap.wait_recv()
-    first_step(1, (1, 7))
     for kind in range(1, 4):
         key_copies[kind, 0].wait_recv()
         to_core(kind, 0)
+    swap.wait_recv()
+    first_step(1, (1, 7))
     for kind in range(1, 4):
         key_copies[kind, 1].wait_recv()
         to_core(kind, 1)
@@ -313,14 +313,14 @@
     wait_core(2)
     finish(y_hi, prompt_a, True)
     scatter(0, y_hi, x_hi)
+    finish(1 - y_hi, prompt_b, False)
+    scatter(1, 1 - y_hi, 1 - x_hi)
     for slot in range(NZ - 1):
         target = place(x, y, (z + RELATIVE[slot]) % NZ, c)
         zs_copies.append(send(
             part.at[y_hi, 1 - x_hi, pl.ds(16 * slot, 16)], zs.at[slot], zs_send.at[slot, 0], zs_recv.at[slot, 0], target))
         zs_copies.append(send(
             zs_stat_src.at[1 - x_hi, slot], zs_stat.at[slot], zs_send.at[slot, 1], zs_recv.at[slot, 1], target))
-    finish(1 - y_hi, prompt_b, False)
-    scatter(1, 1 - y_hi, 1 - x_hi)
 
     rs2_copies = []
 

time: 41.5 us -> 41.7 us (level)
  no operation moved by 1% of the time
where the time goes in v10:
time: 41.7 us; the launch traced here: 41.6 us
  Pallas kernels  41 us (98%)
  local copies, waits for them, and re-layouts  0.62 us (1%)
    pallas_call x1, Pallas kernels, body(): pl.pallas_call(kernel, out_shape=pltpu.VMEM((8, 16, VDIM), BF16), in_spec...  41 us

profile of v10, /device:TPU:8, one launch (start us, length us, event | category | flops | bytes accessed | tf_op | source)
XLA Modules:
  0.0 41.6 jit_solution(4000006447298886098)
XLA Ops:
  0.0 41.0 %shard_map.73 = bf16[8,16,128]{2,1,0:T(8,128)(2,1)S(1)} custom-call(s32[32]{0:T(128)} %parents_hbm.1, s32[32]{0:T(128)} %lengths_hbm.1, s32[32,64]{1,0:T(8,128)} %lists_hbm.1, bf16[32,4,576]{2,1,0:T(4,128)(2,1)} %queries.1, bf16[4,576,128]{2,1,0:T(8,128)(2,1)} %bitcast.3, bf16[2,64,576]{2,1,0:T(8,128)(2,1)} %pool.1, bf16[4,512,128]{2,1,0:T(8,128)(2,1)} %value_up.1), custom_call_target="tpu_custom_call" | custom-call | tf_op jit(solution)/shard_map/pallas_call | solution.py:385
  41.0 0.6 %copy.9 = bf16[32,4,128]{2,1,0:T(4,128)(2,1)} copy(bf16[32,4,128]{2,1,0:T(4,128)(2,1)S(1)} %bitcast.2) | data formatting | bytes 65536

commit v11 on v10

--- a/solution.py
+++ b/solution.py
@@ -313,14 +313,14 @@
     wait_core(2)
     finish(y_hi, prompt_a, True)
     scatter(0, y_hi, x_hi)
-    finish(1 - y_hi, prompt_b, False)
-    scatter(1, 1 - y_hi, 1 - x_hi)
     for slot in range(NZ - 1):
         target = place(x, y, (z + RELATIVE[slot]) % NZ, c)
         zs_copies.append(send(
             part.at[y_hi, 1 - x_hi, pl.ds(16 * slot, 16)], zs.at[slot], zs_send.at[slot, 0], zs_recv.at[slot, 0], target))
         zs_copies.append(send(
             zs_stat_src.at[1 - x_hi, slot], zs_stat.at[slot], zs_send.at[slot, 1], zs_recv.at[slot, 1], target))
+    finish(1 - y_hi, prompt_b, False)
+    scatter(1, 1 - y_hi, 1 - x_hi)
 
     rs2_copies = []
 

time: 41.7 us -> 41.8 us (level)
  no operation moved by 1% of the time
where the time goes in v11:
time: 41.8 us; the launch traced here: 41.7 us
  Pallas kernels  41 us (98%)
  local copies, waits for them, and re-layouts  0.62 us (1%)
    pallas_call x1, Pallas kernels, body(): pl.pallas_call(kernel, out_shape=pltpu.VMEM((8, 16, VDIM), BF16), in_spec...  41 us

profile of v11, /device:TPU:8, one launch (start us, length us, event | category | flops | bytes accessed | tf_op | source)
XLA Modules:
  0.0 41.7 jit_solution(10311366154348876947)
XLA Ops:
  0.0 41.0 %shard_map.73 = bf16[8,16,128]{2,1,0:T(8,128)(2,1)S(1)} custom-call(s32[32]{0:T(128)} %parents_hbm.1, s32[32]{0:T(128)} %lengths_hbm.1, s32[32,64]{1,0:T(8,128)} %lists_hbm.1, bf16[32,4,576]{2,1,0:T(4,128)(2,1)} %queries.1, bf16[4,576,128]{2,1,0:T(8,128)(2,1)} %bitcast.3, bf16[2,64,576]{2,1,0:T(8,128)(2,1)} %pool.1, bf16[4,512,128]{2,1,0:T(8,128)(2,1)} %value_up.1), custom_call_target="tpu_custom_call" | custom-call | tf_op jit(solution)/shard_map/pallas_call | solution.py:385
  41.1 0.6 %copy.9 = bf16[32,4,128]{2,1,0:T(4,128)(2,1)} copy(bf16[32,4,128]{2,1,0:T(4,128)(2,1)S(1)} %bitcast.2) | data formatting | bytes 65536
